TPU v7x, 128 devices: a whole 4x4x4 slice. The times are simulated.
128 devices in a mesh: gx: 8 (over x, core), gy: 16 (over z, y).
Axes of the slice: x: 4, y: 4, z: 4, core: 2. Of those that a mesh axis runs over, the one named last changes fastest.
Arguments:
- normed: bfloat16 [3072, 8192], P('gy', 'gx'), may hold values from -6 to 6
- qkv_weight: bfloat16 [8192, 10240], P('gx', 'gy'), may hold values from -0.0625 to 0.0625
- out_weight: bfloat16 [8192, 8192], P('gy', 'gx'), may hold values from -0.5 to 0.5
- prompt_key_value: bfloat16 [384, 1280, 2048], P(('gx', 'gy')), may hold values from -460 to 460
- beam_key_value: bfloat16 [3072, 48, 2048], P(('gx', 'gy')), may hold values from -6 to 6
- parents: int32 [3072], P(('gx', 'gy')), may hold values from 0 to 7
- lengths: int32 [384], P(('gx', 'gy')), may hold values from 160 to 1280, as said below
Outputs:
- attn_out: bfloat16 [3072, 8192], P('gy', 'gx')
- latest_key_value: bfloat16 [3072, 2048], P(('gx', 'gy'))
Inputs may be any that keep to these rules, and one draw needn't show every extreme that they name: parents numbers a beam within its prompt's 8 beams. `lengths`: some prompt has exactly 1280 cached tokens and some other exactly 160.
All inputs are finite; a program needn't handle non-finite values.
Results may differ from a plain program's by a relative error of at most 0.015.
Values may be sent and summed in bfloat16 or wider, within the bound.
No kernel may reach another device: no remote copies, remote signals or barrier semaphores. Data moves between devices by JAX's collectives and lax.ppermute only.
A program may use at most 128 MiB of HBM per device.

v0:
```python
import jax
import jax.numpy as jnp
from jax import lax
from jax.sharding import PartitionSpec as P

QUERY_HEADS = 64
KEY_HEADS = 8
HEAD_SIZE = 128
BEAMS_PER_PROMPT = 8


def rotary_tables(positions):
    half_dim = HEAD_SIZE // 2
    exponent = 2.0 * jnp.arange(half_dim, dtype=jnp.float32) / HEAD_SIZE
    frequency = jnp.exp(-jnp.log(jnp.float32(500000.0)) * exponent)
    angles = positions.astype(jnp.float32)[:, None] * frequency[None, :]
    return (jnp.cos(angles), jnp.sin(angles))


def rotate(values, cosine, sine_table):
    half_dim = HEAD_SIZE // 2
    leading = values[..., :half_dim]
    trailing = values[..., half_dim:]
    return jnp.concatenate(
        [leading * cosine - trailing * sine_table, trailing * cosine + leading * sine_table],
        axis=-1,
    )


def attend(query_key_value, prompt_key_value, beam_key_value, parents, lengths):
    prompt_beams = query_key_value.shape[0]
    present_prompts = prompt_key_value.shape[0]
    prompt_context = prompt_key_value.shape[1]
    generated_tokens = beam_key_value.shape[1]
    query_groups = QUERY_HEADS // KEY_HEADS
    query_rows = query_key_value[:, : QUERY_HEADS * HEAD_SIZE].reshape(
        prompt_beams, QUERY_HEADS, HEAD_SIZE
    )
    latest_keys = query_key_value[
        :, QUERY_HEADS * HEAD_SIZE : (QUERY_HEADS + KEY_HEADS) * HEAD_SIZE
    ].reshape(prompt_beams, KEY_HEADS, HEAD_SIZE)
    latest_values = query_key_value[:, (QUERY_HEADS + KEY_HEADS) * HEAD_SIZE :]
    positions = jnp.repeat(lengths, BEAMS_PER_PROMPT) + generated_tokens
    cosine, sine_table = rotary_tables(positions)
    rotated_query_rows = rotate(
        query_rows.astype(jnp.float32), cosine[:, None, :], sine_table[:, None, :]
    ).astype(jnp.bfloat16)
    rotated_key_rows = rotate(
        latest_keys.astype(jnp.float32), cosine[:, None, :], sine_table[:, None, :]
    ).astype(jnp.bfloat16)
    fresh_key_value = jnp.concatenate(
        [rotated_key_rows.reshape(prompt_beams, KEY_HEADS * HEAD_SIZE), latest_values], axis=1
    )
    source = (
        jnp.arange(prompt_beams, dtype=jnp.int32) // BEAMS_PER_PROMPT * BEAMS_PER_PROMPT + parents
    )
    beam_history = jnp.take(beam_key_value, source, axis=0)
    grouped_queries = rotated_query_rows.reshape(
        present_prompts, BEAMS_PER_PROMPT, KEY_HEADS, query_groups, HEAD_SIZE
    )
    prompt_cache_keys = prompt_key_value[:, :, : KEY_HEADS * HEAD_SIZE].reshape(
        present_prompts, prompt_context, KEY_HEADS, HEAD_SIZE
    )
    prompt_cache_values = prompt_key_value[:, :, KEY_HEADS * HEAD_SIZE :].reshape(
        present_prompts, prompt_context, KEY_HEADS, HEAD_SIZE
    )
    earlier_keys = beam_history[:, :, : KEY_HEADS * HEAD_SIZE].reshape(
        present_prompts, BEAMS_PER_PROMPT, generated_tokens, KEY_HEADS, HEAD_SIZE
    )
    earlier_values = beam_history[:, :, KEY_HEADS * HEAD_SIZE :].reshape(
        present_prompts, BEAMS_PER_PROMPT, generated_tokens, KEY_HEADS, HEAD_SIZE
    )
    beam_own_keys = rotated_key_rows.reshape(
        present_prompts, BEAMS_PER_PROMPT, KEY_HEADS, HEAD_SIZE
    )
    beam_own_values = latest_values.reshape(present_prompts, BEAMS_PER_PROMPT, KEY_HEADS, HEAD_SIZE)
    scaling = HEAD_SIZE ** (-0.5)
    cache_scores = (
        jnp.einsum(
            "pbgrd,ptgd->pbgrt",
            grouped_queries,
            prompt_cache_keys,
            preferred_element_type=jnp.float32,
        )
        * scaling
    )
    past_scores = (
        jnp.einsum(
            "pbgrd,pbsgd->pbgrs", grouped_queries, earlier_keys, preferred_element_type=jnp.float32
        )
        * scaling
    )
    own_scores = (
        jnp.einsum(
            "pbgrd,pbgd->pbgr", grouped_queries, beam_own_keys, preferred_element_type=jnp.float32
        )
        * scaling
    )
    usable = (jnp.arange(prompt_context, dtype=jnp.int32)[None, :] < lengths[:, None])[
        :, None, None, None, :
    ]
    highest = jnp.maximum(
        jnp.max(jnp.where(usable, cache_scores, -jnp.inf), axis=-1), jnp.max(past_scores, axis=-1)
    )
    highest = jnp.maximum(highest, own_scores)
    cache_terms = jnp.where(usable, jnp.exp(cache_scores - highest[..., None]), 0.0)
    past_terms = jnp.exp(past_scores - highest[..., None])
    own_terms = jnp.exp(own_scores - highest)
    total = jnp.sum(cache_terms, axis=-1) + jnp.sum(past_terms, axis=-1) + own_terms
    cache_weights = (cache_terms / total[..., None]).astype(jnp.bfloat16)
    past_weights = (past_terms / total[..., None]).astype(jnp.bfloat16)
    own_weights = (own_terms / total).astype(jnp.bfloat16)
    attended = jnp.einsum(
        "pbgrt,ptgd->pbgrd", cache_weights, prompt_cache_values, preferred_element_type=jnp.float32
    )
    attended = attended + jnp.einsum(
        "pbgrs,pbsgd->pbgrd", past_weights, earlier_values, preferred_element_type=jnp.float32
    )
    attended = (
        attended
        + own_weights.astype(jnp.float32)[..., None]
        * beam_own_values.astype(jnp.float32)[:, :, :, None, :]
    )
    return (
        attended.reshape(prompt_beams, QUERY_HEADS * HEAD_SIZE).astype(jnp.bfloat16),
        fresh_key_value,
    )


def body(normed, qkv_weight, out_weight, prompt_key_value, beam_key_value, parents, lengths):
    prompt_beams = beam_key_value.shape[0]
    columns = qkv_weight.shape[1]
    groups_x = lax.axis_size("gx")
    groups_y = lax.axis_size("gy")
    partial_qkv = jnp.dot(
        lax.all_gather(normed, "gy", axis=0, tiled=True),
        qkv_weight,
        preferred_element_type=jnp.float32,
    )
    summed = lax.psum_scatter(partial_qkv, "gx", scatter_dimension=0, tiled=True)
    packed = summed.astype(jnp.bfloat16).reshape(groups_y, prompt_beams, columns)
    arrived = lax.all_to_all(packed, "gy", split_axis=0, concat_axis=2, tiled=True)
    query_key_value = arrived.reshape(prompt_beams, groups_y * columns)
    attended, fresh_key_value = attend(
        query_key_value, prompt_key_value, beam_key_value, parents, lengths
    )
    width = out_weight.shape[0]
    pieces = attended.reshape(prompt_beams, groups_y, width)
    copies = jnp.broadcast_to(pieces[:, None, :, :], (prompt_beams, groups_x, groups_y, width))
    copies = copies.reshape(prompt_beams, groups_x * groups_y, width)
    spread = lax.all_to_all(copies, ("gx", "gy"), split_axis=1, concat_axis=0, tiled=True)
    beam_rows = spread.reshape(-1, width)
    result = lax.psum_scatter(
        jnp.dot(beam_rows, out_weight, preferred_element_type=jnp.float32),
        "gy",
        scatter_dimension=0,
        tiled=True,
    )
    return (result.astype(jnp.bfloat16), fresh_key_value)


def solution(mesh):
    return jax.shard_map(
        body,
        mesh=mesh,
        in_specs=(
            P("gy", "gx"),
            P("gx", "gy"),
            P("gy", "gx"),
            P(("gx", "gy"), None, None),
            P(("gx", "gy"), None, None),
            P(("gx", "gy")),
            P(("gx", "gy")),
        ),
        out_specs=(P("gy", "gx"), P(("gx", "gy"), None)),
        check_vma=False,
    )
```

profile of v0, /device:TPU:1, one launch (start us, length us, event | category | flops | bytes accessed | tf_op | source)
XLA Modules:
  0.0 354.1 jit_solution(12245675903520989810)
XLA Ops:
  7.2 0.7 all-gather.2.cloned.1.call-update
  8.0 66.8 %all-gather.2.cloned.1.call-done = bf16[3072,1024]{1,0:T(8,128)(2,1)} async-done(((bf16[192,1024]{1,0:T(8,128)(2,1)}), bf16[3072,1024]{1,0:T(8,128)(2,1)}) %all-gather.2.cloned.1.call-update) | async-done | bytes 6291472 | tf_op jit(solution)/shard_map/all_gather | solution.py:136
  74.8 9.5 %fusion.41 = f32[3072,640]{1,0:T(8,128)} fusion(bf16[3072,1024]{1,0:T(8,128)(2,1)} %all-gather.2.cloned.1.call-done, bf16[1024,640]{1,0:T(8,128)(2,1)S(1)} %copy-done), kind=kOutput, calls=%fused_computation.68 | convolution fusion | flops 4026531840 | bytes 15466496 | tf_op jit(solution)/shard_map/dot_general | solution.py:135
  84.3 0.6 copy-done.4
  85.1 5.5 %gather_fusion = bf16[24,48,2048]{2,1,0:T(8,128)(2,1)} fusion(bf16[24,48,2048]{2,1,0:T(8,128)(2,1)} %param.11, s32[1024]{0:T(1024)S(1)} %pad_clamp_fusion), kind=kCustom, calls=%fused_computation | custom fusion | bytes 9437280 | tf_op jit(solution)/shard_map/jit(_take)/gather | solution.py:57
  90.6 2.9 broadcast_select_fusion
  93.5 2.8 fusion.38
  96.3 12.1 %fusion.37 = (bf16[3,1280,1024]{2,1,0:T(8,128)(2,1)}, bf16[3,1280,1024]{2,1,0:T(8,128)(2,1)}) fusion(bf16[3,1280,2048]{2,1,0:T(8,128)(2,1)} %param.10), kind=kLoop, calls=%fused_computation.64 | loop fusion | bytes 31457280 | tf_op jit(solution)/shard_map/slice | solution.py:61
  108.4 25.0 %reduce-scatter.3.cloned.1.call-done = f32[384,640]{1,0:T(8,128)} async-done(((f32[3072,640]{1,0:T(8,128)}), f32[384,640]{1,0:T(8,128)}) %reduce-scatter.3.cloned.1.call-update) | async-done | bytes 983056 | tf_op jit(solution)/shard_map/reduce_scatter | solution.py:140
  133.4 2.1 convert_element_type.69
  135.4 6.7 %all-to-all-start = ((bf16[16,24,640]{2,1,0:T(8,128)(2,1)}), bf16[16,24,640]{2,1,0:T(8,128)(2,1)S(1)}, u32[]{:S(2)}, u32[]{:S(2)}) async-start(bf16[16,24,640]{2,1,0:T(8,128)(2,1)} %bitcast), calls=%async_computation.1 | async-start | bytes 983040 | tf_op jit(solution)/shard_map/all_to_all | solution.py:142
  142.5 10.8 %copy.75 = bf16[3,1280,1024]{1,2,0:T(8,128)(2,1)} copy(bf16[3,1280,1024]{2,1,0:T(8,128)(2,1)} %get-tuple-element.6) | data formatting | bytes 15728640
  153.4 3.8 %copy.79 = bf16[144,8,8,128]{3,2,1,0:T(8,128)(2,1)} copy(bf16[144,8,8,128]{3,1,2,0:T(8,128)(2,1)} %bitcast.95) | data formatting | bytes 4718592
  157.2 10.8 %copy.76 = bf16[3,1280,1024]{1,2,0:T(8,128)(2,1)} copy(bf16[3,1280,1024]{2,1,0:T(8,128)(2,1)} %get-tuple-element.7) | data formatting | bytes 15728640
  168.0 3.8 %copy.81 = bf16[144,8,8,128]{3,2,1,0:T(8,128)(2,1)} copy(bf16[144,8,8,128]{3,1,2,0:T(8,128)(2,1)} %bitcast.94) | data formatting | bytes 4718592
  172.3 0.4 subtract_convert_fusion
  173.0 0.3 fusion.29
  173.4 3.1 fusion.40
  176.4 5.0 %fusion = (f32[3,8,8,8]{3,1,2,0:T(8,128)S(1)}, f32[3,8,8,8,1280]{4,3,2,1,0:T(8,128)S(1)}) fusion(pred[3,1280]{1,0:T(4,128)(4,1)S(1)} %iota_compare_fusion, bf16[3,1280,8,128,1]{1,3,4,2,0:T(8,128)(2,1)} %bitcast.91, bf16[3,8,8,8,128]{4,3,2,1,0:T(8,128)(2,1)S(1)} %pad_maximum_fusion), kind=kOutput, calls=%fused_computation.3 | convolution fusion | flops 509213184 | bytes 16131840 | tf_op jit(solution)/shard_map/pbgrd,ptgd->pbgrt/dot_general | solution.py:79
  181.5 3.0 copy-done.2
  184.5 1.9 fusion.3
  186.4 0.5 fusion.23
  187.0 9.9 %fusion.19 = f32[3,8,8,8,128]{4,3,1,2,0:T(8,128)S(1)} fusion(bf16[3,1280,8,128,1]{1,3,4,2,0:T(8,128)(2,1)} %bitcast.96, f32[3,8,8,8,1280]{4,3,2,1,0:T(8,128)} %copy-done.2, f32[3,8,8,8]{3,1,2,0:T(8,128)S(1)} %get-tuple-element.3, f32[3,8,8,8]{3,1,2,0:T(8,128)S(1)} %fusion.28, pred[3,1280]{1,0:T(4,128)(4,1)S(1)} %iota_compare_fusion), kind=kOutput, calls=%fused_computation.18 | convolution fusion | flops 513146880 | bytes 16531200 | tf_op jit(solution)/shard_map/pbgrt,ptgd->pbgrd/dot_general | solution.py:113
  196.9 1.2 fusion.20
  198.2 0.2 convert_element_type.83
  198.5 0.2 copy.61
  198.7 0.3 broadcast_in_dim.60
  199.0 48.4 %all_to_all.30 = bf16[24,128,512]{2,0,1:T(8,128)(2,1)S(1)} all-to-all(bf16[24,128,512]{2,0,1:T(8,128)(2,1)S(1)} %bitcast.92), channel_id=1, replica_groups=mesh['gx'=8,'gy'=16] {'gx','gy'}, dimensions={1} | all-to-all | bytes 6291456 | tf_op jit(solution)/shard_map/all_to_all | solution.py:151
  247.4 6.3 %fusion.42 = f32[3072,1024]{1,0:T(8,128)} fusion(bf16[3072,512]{1,0:T(8,128)(2,1)S(1)} %bitcast.98, bf16[512,1024]{1,0:T(8,128)(2,1)S(1)} %copy-done.5), kind=kOutput, calls=%fused_computation.69 | convolution fusion | flops 3221225472 | bytes 16777216 | tf_op jit(solution)/shard_map/dot_general | solution.py:154
  253.9 0.6 pad_maximum_fusion.1
  254.5 91.1 %reduce-scatter.5.cloned.1.call-done = f32[192,1024]{1,0:T(8,128)} async-done(((f32[3072,1024]{1,0:T(8,128)}), f32[192,1024]{1,0:T(8,128)}) %reduce-scatter.5.cloned.1.call-update) | async-done | bytes 786448 | tf_op jit(solution)/shard_map/reduce_scatter | solution.py:153
  345.6 1.9 convert_element_type.84
  (41 shorter events, 1.8 us)
Async XLA Ops:
  7.2 67.7 %copy-start = (bf16[1024,640]{1,0:T(8,128)(2,1)S(1)}, bf16[1024,640]{1,0:T(8,128)(2,1)}, u32[]{:S(2)}) copy-start(bf16[1024,640]{1,0:T(8,128)(2,1)} %param.8) | copy-start | bytes 3932164
  7.2 67.6 %all-gather.2.cloned.1.call-start = ((), (), s32[]{:S(2)}) async-start(), calls=%async_computation.4 | async-start | bytes 6684672 | tf_op jit(solution)/shard_map/all_gather | solution.py:136
  7.9 125.5 %reduce-scatter.3.cloned.1.call-start = ((), (), s32[]{:S(2)}) async-start(), calls=%async_computation.5 | async-start | bytes 8847360 | tf_op jit(solution)/shard_map/reduce_scatter | solution.py:140
  84.3 0.7 copy-start.4
  84.3 0.8 copy-start.6
  135.4 36.4 %all-to-all-start = ((bf16[16,24,640]{2,1,0:T(8,128)(2,1)}), bf16[16,24,640]{2,1,0:T(8,128)(2,1)S(1)}, u32[]{:S(2)}, u32[]{:S(2)}) async-start(bf16[16,24,640]{2,1,0:T(8,128)(2,1)} %bitcast), calls=%async_computation.1 | async-start | bytes 983040 | tf_op jit(solution)/shard_map/all_to_all | solution.py:142
  142.2 203.4 %reduce-scatter.5.cloned.1.call-start = ((), (), s32[]{:S(2)}) async-start(), calls=%async_computation.6 | async-start | bytes 13369344 | tf_op jit(solution)/shard_map/reduce_scatter | solution.py:153
  181.4 3.1 copy-start.2
  187.0 9.9 %copy-start.3 = (bf16[144,8,8,128]{3,2,1,0:T(8,128)(2,1)S(1)}, bf16[144,8,8,128]{3,2,1,0:T(8,128)(2,1)}, u32[]{:S(2)}) copy-start(bf16[144,8,8,128]{3,2,1,0:T(8,128)(2,1)} %copy.81) | copy-start | bytes 7077892
  198.1 49.3 %copy-start.5 = (bf16[512,1024]{1,0:T(8,128)(2,1)S(1)}, bf16[512,1024]{1,0:T(8,128)(2,1)}, u32[]{:S(2)}) copy-start(bf16[512,1024]{1,0:T(8,128)(2,1)} %param.9) | copy-start | bytes 3145732
  253.7 93.8 %copy-start.1 = (bf16[1024,640]{1,0:T(8,128)(2,1)S(1)}, bf16[1024,640]{1,0:T(8,128)(2,1)}, u32[]{:S(2)}) copy-start(bf16[1024,640]{1,0:T(8,128)(2,1)} %param.8) | copy-start | bytes 3932164
Sparse Core Ops, SparseCore 0:
  10.2 64.6 all-gather.1
  84.4 48.9 reduce-scatter.2
  253.9 91.6 reduce-scatter.4
where the time goes:
time: 355 us; the launch traced here: 354 us
  waiting for transfers between devices  184 us (52%)
  local copies, waits for them, and re-layouts  54.5 us (15%)
  blocking collectives  48.4 us (14%)
  matrix products  35.3 us (10%)
  between operations  14 us (4%)
  other arithmetic  11.2 us (3%)
  starting transfers between devices  7.02 us (2%)
    reduce_scatter x1, waiting for transfers between devices, body(): lax.psum_scatter(jnp.dot(beam_rows, out_weight, preferred_element_type=jn...  91.1 us
    all_gather x1, waiting for transfers between devices, body(): lax.all_gather(normed, 'gy', axis=0, tiled=True)  66.8 us
    all_to_all x1, blocking collectives, body(): lax.all_to_all(copies, ('gx', 'gy'), split_axis=1, concat_axis=0, tiled=T...  48.4 us
    unnamed x22, local copies, waits for them, and re-layouts  33.1 us
    reduce_scatter x1, waiting for transfers between devices, body(): lax.psum_scatter(partial_qkv, 'gx', scatter_dimension=0, tiled=True)  25 us
    slice x1, local copies, waits for them, and re-layouts, attend(): prompt_key_value[:, :, :KEY_HEADS * HEAD_SIZE]  12.1 us
    dot_general x1, matrix products, attend(): jnp.einsum('pbgrt,ptgd->pbgrd', cache_weights, prompt_cache_values, prefe...  9.85 us
    dot_general x1, matrix products, body(): jnp.dot(lax.all_gather(normed, 'gy', axis=0, tiled=True), qkv_weight, pre...  9.46 us
  transfers between devices with their start and end apart: 4, of which 3 were waited for; matrix products, arithmetic and copies ran while one was open for 15% of the time, Pallas kernels for 0%

commit v1 on v0

v1 whole, which is shorter than its diff:
```python
import functools

import jax
import jax.numpy as jnp
from jax import lax
from jax.experimental import pallas as pl
from jax.experimental.pallas import tpu as pltpu
from jax.sharding import Mesh
from jax.sharding import PartitionSpec as P

QUERY_HEADS = 64
KEY_HEADS = 8
HEAD_SIZE = 128
BEAMS_PER_PROMPT = 8
MASKED = -1e30


def rotary_tables(positions):
    half_dim = HEAD_SIZE // 2
    exponent = 2.0 * jnp.arange(half_dim, dtype=jnp.float32) / HEAD_SIZE
    frequency = jnp.exp(-jnp.log(jnp.float32(500000.0)) * exponent)
    angles = positions.astype(jnp.float32)[:, None] * frequency[None, :]
    cosine, sine = jnp.cos(angles), jnp.sin(angles)
    return (
        jnp.concatenate([cosine, cosine], axis=1)[:, None, :],
        jnp.concatenate([-sine, sine], axis=1)[:, None, :],
    )


def attend_kernel(
    prompt, parents_ref, lengths_ref, terms_ref, cos_ref, sin_ref, pkv_ref, bkv_ref, out_ref, fresh_ref
):
    beams, size = BEAMS_PER_PROMPT, HEAD_SIZE
    ratio = QUERY_HEADS // KEY_HEADS
    rows = beams * ratio
    context = pkv_ref.shape[1]
    past = bkv_ref.shape[0]
    generated = past // beams
    length = lengths_ref[prompt]
    cosine = jnp.broadcast_to(cos_ref[0], (beams, size))
    sine = jnp.broadcast_to(sin_ref[0], (beams, size))
    scale = size ** (-0.5) * 1.4426950408889634
    held = terms_ref.shape[-1] // size
    given = out_ref.shape[-1] // size

    def head(h):
        at = slice((h % held) * size, (h % held + 1) * size)
        total = terms_ref[0, h // held, :, at].astype(jnp.float32)
        for i in range(1, terms_ref.shape[0]):
            total = total + terms_ref[i, h // held, :, at].astype(jnp.float32)
        return total.astype(jnp.bfloat16).astype(jnp.float32)

    def rotated(v):
        v = v * cosine + pltpu.roll(v, size // 2, 1) * sine
        return v.astype(jnp.bfloat16).astype(jnp.float32)

    usable = lax.broadcasted_iota(jnp.int32, (rows, context), 1) < length
    beam = lax.rem(lax.broadcasted_iota(jnp.int32, (rows, past), 0), beams)
    first = jnp.zeros((rows, past), jnp.int32)
    for b in range(beams):
        first = jnp.where(beam == b, parents_ref[prompt * beams + b] * generated, first)
    place = lax.broadcasted_iota(jnp.int32, (rows, past), 1)
    chosen = (place >= first) & (place < first + generated)
    across = (((1,), (1,)), ((), ()))
    along = (((1,), (0,)), ((), ()))
    for g in range(KEY_HEADS):
        ks = slice(g * size, (g + 1) * size)
        vs = slice((KEY_HEADS + g) * size, (KEY_HEADS + g + 1) * size)
        q = jnp.concatenate([rotated(head(g * ratio + r)) for r in range(ratio)], axis=0)
        own_key = rotated(head(QUERY_HEADS + g))
        own_value = head(QUERY_HEADS + KEY_HEADS + g)
        fresh_ref[:, ks] = own_key.astype(jnp.bfloat16)
        fresh_ref[:, vs] = own_value.astype(jnp.bfloat16)
        qb = q.astype(jnp.bfloat16)
        s1 = lax.dot_general(qb, pkv_ref[0, :, ks], across, preferred_element_type=jnp.float32)
        s2 = lax.dot_general(qb, bkv_ref[:, ks], across, preferred_element_type=jnp.float32)
        s3 = jnp.sum(q * jnp.concatenate([own_key] * ratio, axis=0), axis=1, keepdims=True)
        s1 = jnp.where(usable, s1, MASKED)
        s2 = jnp.where(chosen, s2, MASKED)
        top = jnp.maximum(jnp.max(s1, axis=1, keepdims=True), jnp.max(s2, axis=1, keepdims=True))
        top = jnp.maximum(top, s3)
        e1 = jnp.exp2((s1 - top) * scale)
        e2 = jnp.exp2((s2 - top) * scale)
        e3 = jnp.exp2((s3 - top) * scale)
        total = jnp.sum(e1, axis=1, keepdims=True) + jnp.sum(e2, axis=1, keepdims=True) + e3
        o = lax.dot_general(
            e1.astype(jnp.bfloat16), pkv_ref[0, :, vs], along, preferred_element_type=jnp.float32
        )
        o = o + lax.dot_general(
            e2.astype(jnp.bfloat16), bkv_ref[:, vs], along, preferred_element_type=jnp.float32
        )
        o = (o + e3 * jnp.concatenate([own_value] * ratio, axis=0)) / total
        for r in range(ratio):
            h = g * ratio + r
            at = slice((h % given) * size, (h % given + 1) * size)
            out_ref[h // given, :, at] = o[r * beams : (r + 1) * beams].astype(jnp.bfloat16)


def attend(prompt, terms, cosine, sine, pkv, bkv, parents, lengths):
    prompts, context, width = pkv.shape
    past = bkv.shape[0] // prompts
    slabs = terms.shape[1]
    given = QUERY_HEADS * HEAD_SIZE // slabs
    grid_spec = pltpu.PrefetchScalarGridSpec(
        num_scalar_prefetch=2,
        grid=(1,),
        in_specs=[
            pl.BlockSpec(terms.shape, lambda i, *_: (0, 0, 0, 0)),
            pl.BlockSpec((1, 1, HEAD_SIZE), lambda i, *_: (prompt, 0, 0)),
            pl.BlockSpec((1, 1, HEAD_SIZE), lambda i, *_: (prompt, 0, 0)),
            pl.BlockSpec((1, context, width), lambda i, *_: (prompt, 0, 0)),
            pl.BlockSpec((past, width), lambda i, *_: (prompt, 0)),
        ],
        out_specs=[
            pl.BlockSpec((slabs, BEAMS_PER_PROMPT, given), lambda i, *_: (0, 0, 0)),
            pl.BlockSpec((BEAMS_PER_PROMPT, width), lambda i, *_: (0, 0)),
        ],
    )
    return pl.pallas_call(
        functools.partial(attend_kernel, prompt),
        grid_spec=grid_spec,
        out_shape=[
            jax.ShapeDtypeStruct((slabs, BEAMS_PER_PROMPT, given), jnp.bfloat16),
            jax.ShapeDtypeStruct((BEAMS_PER_PROMPT, width), jnp.bfloat16),
        ],
        compiler_params=pltpu.CompilerParams(vmem_limit_bytes=32 * 1024 * 1024),
        cost_estimate=pl.CostEstimate(
            flops=4 * 64 * HEAD_SIZE * KEY_HEADS * (context + past),
            bytes_accessed=2 * width * (context + past),
            transcendentals=64 * KEY_HEADS * (context + past),
        ),
    )(parents, lengths, terms, cosine, sine, pkv, bkv)


SWAP = [(0, 1), (1, 0)]


def body(normed, qkv_weight, out_weight, prompt_key_value, beam_key_value, parents, lengths):
    prompts = prompt_key_value.shape[0]
    beams = BEAMS_PER_PROMPT
    nx, nz, ny = lax.axis_size("x"), lax.axis_size("z"), lax.axis_size("y")
    core = lax.axis_index("core")
    slabs = nz * ny
    depth, columns = qkv_weight.shape
    width = out_weight.shape[0]
    plane = ("x", "z", "y")
    cosine, sine = rotary_tables(lengths + beam_key_value.shape[1])
    history = beam_key_value.reshape(-1, beam_key_value.shape[-1])
    parts = normed.reshape(-1, prompts, beams, depth)
    results, fresh = [], []
    for c in range(prompts):
        rows = lax.all_gather(parts[:, c].reshape(-1, depth), ("z", "y"), axis=0, tiled=True)
        terms = jnp.dot(rows, qkv_weight, preferred_element_type=jnp.float32)
        terms = terms.reshape(nx, 2, slabs, beams, columns)
        away = lax.dynamic_index_in_dim(terms, 1 - core, 1, keepdims=False).astype(jnp.bfloat16)
        mine = lax.dynamic_index_in_dim(terms, core, 1, keepdims=False)
        mine = (mine + lax.ppermute(away, "core", SWAP).astype(jnp.float32)).astype(jnp.bfloat16)
        mine = mine.reshape(nx * slabs, beams, columns)
        arrived = lax.all_to_all(mine, plane, split_axis=0, concat_axis=0, tiled=True)
        arrived = arrived.reshape(nx, slabs, beams, columns)
        out, new = attend(
            c, arrived, cosine, sine, prompt_key_value, history, parents, lengths
        )
        fresh.append(new)
        copies = jnp.broadcast_to(out[None], (nx,) + out.shape).reshape(nx * slabs, beams, width)
        spread = lax.all_to_all(copies, plane, split_axis=0, concat_axis=0, tiled=True)
        spread = spread.reshape(nx, slabs * beams, width)
        twin = lax.ppermute(spread, "core", SWAP)
        both = jnp.stack(
            [jnp.where(core == 0, spread, twin), jnp.where(core == 0, twin, spread)], axis=1
        )
        product = jnp.dot(
            both.reshape(-1, width), out_weight, preferred_element_type=jnp.float32
        ).astype(jnp.bfloat16)
        result = lax.psum_scatter(product, ("z", "y"), scatter_dimension=0, tiled=True)
        results.append(result.reshape(-1, beams, out_weight.shape[1]))
    result = jnp.stack(results, axis=1).reshape(-1, out_weight.shape[1])
    return (result, jnp.concatenate(fresh, axis=0))


def solution(mesh):
    chips = Mesh(mesh.devices.reshape(4, 2, 4, 4), ("x", "core", "z", "y"))
    gx, gy = ("x", "core"), ("z", "y")
    whole = gx + gy
    return jax.shard_map(
        body,
        mesh=chips,
        in_specs=(
            P(gy, gx),
            P(gx, gy),
            P(gy, gx),
            P(whole, None, None),
            P(whole, None, None),
            P(whole),
            P(whole),
        ),
        out_specs=(P(gy, gx), P(whole, None)),
        check_vma=False,
    )
```

time: 355 us -> 410 us (1.15)
  waiting for transfers between devices: 184 us -> 223 us
  blocking collectives: 48.4 us -> 85.7 us
  local copies, waits for them, and re-layouts: 54.5 us -> 29.5 us
  matrix products: 35.3 us -> 18 us
  Pallas kernels: 0 us -> 13.6 us
  starting transfers between devices: 7.02 us -> 19.3 us
  other arithmetic: 11.2 us -> 5.1 us
    all_to_all x1 -> x5, blocking collectives: 48.4 us -> 85.7 us  [the longest x3 50.1 us: body(): lax.all_to_all(copies, plane, split_axis=0, concat_axis=0, tiled=True)]
    reduce_scatter x2 -> x3, waiting for transfers between devices: 116 us -> 151 us  [body(): lax.psum_scatter(product, ('z', 'y'), scatter_dimension=0, tiled=True)]
    all_gather x1 -> x3, waiting for transfers between devices: 66.8 us -> 47.6 us  [body(): lax.all_gather(parts[:, c].reshape(-1, depth), ('z', 'y'), axis=0, tiled=...]
    dot_general x7 -> x6, matrix products: 35.3 us -> 18 us  [the longest x3 10.2 us: body(): terms = jnp.dot(rows, qkv_weight, preferred_element_type=jnp.float32)]
    slice x2 -> x0, local copies, waits for them, and re-layouts: 14.9 us -> none  [the longest x1 12.1 us: attend(): prompt_key_value[:, :, :KEY_HEADS * HEAD_SIZE]]
    pallas_call x0 -> x3, Pallas kernels: none -> 13.6 us  [attend(): pl.pallas_call(functools.partial(attend_kernel, prompt), grid_spec=grid_s...]
    all_to_all x1, waiting for transfers between devices: 0.01 us -> 13 us  [body(): lax.all_to_all(mine, plane, split_axis=0, concat_axis=0, tiled=True)]
    ppermute x0 -> x6, starting transfers between devices: none -> 11.1 us  [the longest x3 8.39 us: body(): twin = lax.ppermute(spread, 'core', SWAP)]
  transfers between devices with their start and end apart: 4 -> 13, of which waited for: 3 -> 10; matrix products, arithmetic and copies ran while one was open for 15% -> 6% of each run, Pallas kernels for 0% -> 3%
where the time goes in v1:
time: 410 us; the launch traced here: 409 us
  waiting for transfers between devices  223 us (54%)
  blocking collectives  85.7 us (21%)
  local copies, waits for them, and re-layouts  29.5 us (7%)
  starting transfers between devices  19.3 us (5%)
  matrix products  18 us (4%)
  between operations  14.3 us (3%)
  Pallas kernels  13.6 us (3%)
  other arithmetic  5.1 us (1%)
    reduce_scatter x3, waiting for transfers between devices, body(): lax.psum_scatter(product, ('z', 'y'), scatter_dimension=0, tiled=True)  151 us
    all_to_all x3, blocking collectives, body(): lax.all_to_all(copies, plane, split_axis=0, concat_axis=0, tiled=True)  50.1 us
    all_gather x3, waiting for transfers between devices, body(): lax.all_gather(parts[:, c].reshape(-1, depth), ('z', 'y'), axis=0, tiled=...  47.6 us
    all_to_all x2, blocking collectives, body(): lax.all_to_all(mine, plane, split_axis=0, concat_axis=0, tiled=True)  35.6 us
    unnamed x22, local copies, waits for them, and re-layouts  26.4 us
    pallas_call x3, Pallas kernels, attend(): pl.pallas_call(functools.partial(attend_kernel, prompt), grid_spec=grid_s...  13.6 us
    all_to_all x1, waiting for transfers between devices, body(): lax.all_to_all(mine, plane, split_axis=0, concat_axis=0, tiled=True)  13 us
    dot_general x3, matrix products, body(): terms = jnp.dot(rows, qkv_weight, preferred_element_type=jnp.float32)  10.2 us
  transfers between devices with their start and end apart: 13, of which 10 were waited for; matrix products, arithmetic and copies ran while one was open for 6% of the time, Pallas kernels for 3%

profile of v1, /device:TPU:1, one launch (start us, length us, event | category | flops | bytes accessed | tf_op | source)
XLA Modules:
  0.0 408.5 jit_solution(9312412123247430274)
XLA Ops:
  7.2 1.9 slice_bitcast_fusion.2
  10.6 47.6 %all-gather.4.cloned.1.call-done = bf16[1024,1024]{1,0:T(8,128)(2,1)} async-done(((bf16[64,1024]{1,0:T(8,128)(2,1)}), bf16[1024,1024]{1,0:T(8,128)(2,1)}) %all-gather.4.cloned.1.call-update) | async-done | bytes 2097168 | tf_op jit(solution)/shard_map/all_gather | solution.py:152
  58.2 3.4 fusion.7
  63.2 1.8 collective-permute-start
  66.7 2.3 fusion.2
  69.0 8.0 %all-to-all-start = ((bf16[64,8,640]{2,1,0:T(8,128)(2,1)}), bf16[64,8,640]{2,1,0:T(8,128)(2,1)S(1)}, u32[]{:S(2)}, u32[]{:S(2)}) async-start(bf16[64,8,640]{2,1,0:T(8,128)(2,1)} %bitcast.5), calls=%async_computation | async-start | bytes 1310720 | tf_op jit(solution)/shard_map/all_to_all | solution.py:159
  77.4 13.0 %all-to-all-done = bf16[64,8,640]{2,1,0:T(8,128)(2,1)S(1)} async-done(((bf16[64,8,640]{2,1,0:T(8,128)(2,1)}), bf16[64,8,640]{2,1,0:T(8,128)(2,1)S(1)}, u32[]{:S(2)}, u32[]{:S(2)}) %all-to-all-start) | async-done | bytes 655392 | tf_op jit(solution)/shard_map/all_to_all | solution.py:159
  90.4 5.6 %copy-done.1 = bf16[3,1280,2048]{2,1,0:T(8,128)(2,1)S(1)} copy-done((bf16[3,1280,2048]{2,1,0:T(8,128)(2,1)S(1)}, bf16[3,1280,2048]{2,1,0:T(8,128)(2,1)}, u32[]{:S(2)}) %copy-start.1) | copy-done | bytes 15728664
  96.0 2.3 copy-done.4
  98.3 4.5 %shard_map.86 = (bf16[16,8,512]{2,1,0:T(8,128)(2,1)S(1)}, bf16[8,2048]{1,0:T(8,128)(2,1)S(1)}) custom-call(s32[24]{0:T(128)S(1)} %copy-done.7, s32[3]{0:T(128)S(1)} %copy-done.8, bf16[4,16,8,640]{3,2,1,0:T(8,128)(2,1)S(1)} %bitcast.88, f32[3,1,128]{2,1,0:T(1,128)S(1)} %copy.13.cos_ref, f32[3,1,128]{2,1,0:T(1,128)S(1)} %broadcast_in_dim.11.sin_ref, ...), custom_call_target="tpu_custom_call" | custom-call | flops 436207616 | bytes 6815744 | tf_op jit(solution)/shard_map/pallas_call | solution.py:119
  102.9 17.0 %all_to_all.30 = bf16[64,8,512]{2,1,0:T(8,128)(2,1)S(1)} all-to-all(bf16[64,8,512]{2,1,0:T(8,128)(2,1)S(1)} %bitcast.99), channel_id=1, replica_groups=mesh['x'=4,'core'=2,'z'=4,'y'=4] {'x','z','y'}, dimensions={0} | all-to-all | bytes 1048576 | tf_op jit(solution)/shard_map/all_to_all | solution.py:166
  119.8 2.5 collective-permute-start.1
  125.1 2.6 convolution_convert_fusion.2
  127.8 3.4 fusion.8
  131.8 1.7 collective-permute-done.2
  133.6 17.9 %all_to_all.31 = bf16[64,8,640]{2,1,0:T(8,128)(2,1)S(1)} all-to-all(bf16[64,8,640]{2,1,0:T(8,128)(2,1)S(1)} %bitcast.92), channel_id=1, replica_groups=mesh['x'=4,'core'=2,'z'=4,'y'=4] {'x','z','y'}, dimensions={0} | all-to-all | bytes 1310720 | tf_op jit(solution)/shard_map/all_to_all | solution.py:159
  151.5 5.7 %copy-done.2 = bf16[3,1280,2048]{2,1,0:T(8,128)(2,1)S(1)} copy-done((bf16[3,1280,2048]{2,1,0:T(8,128)(2,1)S(1)}, bf16[3,1280,2048]{2,1,0:T(8,128)(2,1)}, u32[]{:S(2)}) %copy-start.2) | copy-done | bytes 15728664
  157.2 2.4 copy-done.5
  159.5 4.5 %shard_map.87 = (bf16[16,8,512]{2,1,0:T(8,128)(2,1)S(1)}, bf16[8,2048]{1,0:T(8,128)(2,1)S(1)}) custom-call(s32[24]{0:T(128)S(1)} %copy-done.7, s32[3]{0:T(128)S(1)} %copy-done.8, bf16[4,16,8,640]{3,2,1,0:T(8,128)(2,1)S(1)} %bitcast.90, f32[3,1,128]{2,1,0:T(1,128)S(1)} %copy.13.cos_ref, f32[3,1,128]{2,1,0:T(1,128)S(1)} %broadcast_in_dim.11.sin_ref, ...), custom_call_target="tpu_custom_call" | custom-call | flops 436207616 | bytes 6815744 | tf_op jit(solution)/shard_map/pallas_call | solution.py:119
  164.1 15.6 %all_to_all.32 = bf16[64,8,512]{2,1,0:T(8,128)(2,1)S(1)} all-to-all(bf16[64,8,512]{2,1,0:T(8,128)(2,1)S(1)} %bitcast.100), channel_id=1, replica_groups=mesh['x'=4,'core'=2,'z'=4,'y'=4] {'x','z','y'}, dimensions={0} | all-to-all | bytes 1048576 | tf_op jit(solution)/shard_map/all_to_all | solution.py:166
  179.7 3.4 collective-permute-start.3
  184.9 2.6 convolution_convert_fusion.1
  187.6 3.4 fusion.9
  193.5 17.7 %all_to_all.33 = bf16[64,8,640]{2,1,0:T(8,128)(2,1)S(1)} all-to-all(bf16[64,8,640]{2,1,0:T(8,128)(2,1)S(1)} %bitcast.91), channel_id=1, replica_groups=mesh['x'=4,'core'=2,'z'=4,'y'=4] {'x','z','y'}, dimensions={0} | all-to-all | bytes 1310720 | tf_op jit(solution)/shard_map/all_to_all | solution.py:159
  211.2 5.6 %copy-done.3 = bf16[3,1280,2048]{2,1,0:T(8,128)(2,1)S(1)} copy-done((bf16[3,1280,2048]{2,1,0:T(8,128)(2,1)S(1)}, bf16[3,1280,2048]{2,1,0:T(8,128)(2,1)}, u32[]{:S(2)}) %copy-start.3) | copy-done | bytes 15728664
  216.8 2.3 copy-done.6
  219.1 4.5 %shard_map.88 = (bf16[16,8,512]{2,1,0:T(8,128)(2,1)S(1)}, bf16[8,2048]{1,0:T(8,128)(2,1)S(1)}) custom-call(s32[24]{0:T(128)S(1)} %copy-done.7, s32[3]{0:T(128)S(1)} %copy-done.8, bf16[4,16,8,640]{3,2,1,0:T(8,128)(2,1)S(1)} %bitcast.89, f32[3,1,128]{2,1,0:T(1,128)S(1)} %copy.13.cos_ref, f32[3,1,128]{2,1,0:T(1,128)S(1)} %broadcast_in_dim.11.sin_ref, ...), custom_call_target="tpu_custom_call" | custom-call | flops 436207616 | bytes 6815744 | tf_op jit(solution)/shard_map/pallas_call | solution.py:119
  223.7 17.6 %all_to_all.34 = bf16[64,8,512]{2,1,0:T(8,128)(2,1)S(1)} all-to-all(bf16[64,8,512]{2,1,0:T(8,128)(2,1)S(1)} %bitcast.101), channel_id=1, replica_groups=mesh['x'=4,'core'=2,'z'=4,'y'=4] {'x','z','y'}, dimensions={0} | all-to-all | bytes 1048576 | tf_op jit(solution)/shard_map/all_to_all | solution.py:166
  241.2 2.5 collective-permute-start.5
  245.5 2.6 convolution_convert_fusion
  248.8 74.2 %reduce-scatter.6.cloned.1.call-done = bf16[64,1024]{1,0:T(8,128)(2,1)} async-done(((bf16[1024,1024]{1,0:T(8,128)(2,1)}), bf16[64,1024]{1,0:T(8,128)(2,1)}) %reduce-scatter.6.cloned.1.call-update) | async-done | bytes 131088 | tf_op jit(solution)/shard_map/reduce_scatter | solution.py:175
  323.0 76.8 %reduce-scatter.8.cloned.1.call-done = bf16[64,1024]{1,0:T(8,128)(2,1)} async-done(((bf16[1024,1024]{1,0:T(8,128)(2,1)}), bf16[64,1024]{1,0:T(8,128)(2,1)}) %reduce-scatter.8.cloned.1.call-update) | async-done | bytes 131088 | tf_op jit(solution)/shard_map/reduce_scatter | solution.py:175
  (64 shorter events, 17.3 us)
Async XLA Ops:
  7.2 51.1 %copy-start = (bf16[1024,640]{1,0:T(8,128)(2,1)S(1)}, bf16[1024,640]{1,0:T(8,128)(2,1)}, u32[]{:S(2)}) copy-start(bf16[1024,640]{1,0:T(8,128)(2,1)} %param.8) | copy-start | bytes 3932164
  7.2 51.0 %all-gather.4.cloned.1.call-start = ((), (), s32[]{:S(2)}) async-start(), calls=%async_computation.9 | async-start | bytes 2228224 | tf_op jit(solution)/shard_map/all_gather | solution.py:152
  9.1 118.7 %all-gather.6.cloned.1.call-start = ((), (), s32[]{:S(2)}) async-start(), calls=%async_computation.11 | async-start | bytes 2228224 | tf_op jit(solution)/shard_map/all_gather | solution.py:152
  9.9 177.7 %all-gather.8.cloned.1.call-start = ((), (), s32[]{:S(2)}) async-start(), calls=%async_computation.13 | async-start | bytes 2228224 | tf_op jit(solution)/shard_map/all_gather | solution.py:152
  61.6 1.5 copy-start.9
  63.2 13.9 %copy-start.8 = (s32[3]{0:T(128)S(1)}, s32[3]{0:T(128)}, u32[]{:S(2)}) copy-start(s32[3]{0:T(128)} %lengths_ref.5) | copy-start | bytes 40
  63.2 27.2 %copy-start.7 = (s32[24]{0:T(128)S(1)}, s32[24]{0:T(128)}, u32[]{:S(2)}) copy-start(s32[24]{0:T(128)} %parents_ref.5) | copy-start | bytes 292
  63.2 3.5 collective-permute-start
  69.0 21.4 %all-to-all-start = ((bf16[64,8,640]{2,1,0:T(8,128)(2,1)}), bf16[64,8,640]{2,1,0:T(8,128)(2,1)S(1)}, u32[]{:S(2)}, u32[]{:S(2)}) async-start(bf16[64,8,640]{2,1,0:T(8,128)(2,1)} %bitcast.5), calls=%async_computation | async-start | bytes 1310720 | tf_op jit(solution)/shard_map/all_to_all | solution.py:159
  77.0 171.8 %reduce-scatter.4.cloned.1.call-start = ((), (), s32[]{:S(2)}) async-start(), calls=%async_computation.10 | async-start | bytes 2228224 | tf_op jit(solution)/shard_map/reduce_scatter | solution.py:175
  90.4 5.6 %copy-start.1 = (bf16[3,1280,2048]{2,1,0:T(8,128)(2,1)S(1)}, bf16[3,1280,2048]{2,1,0:T(8,128)(2,1)}, u32[]{:S(2)}) copy-start(bf16[3,1280,2048]{2,1,0:T(8,128)(2,1)} %pkv_ref.5) | copy-start | bytes 47185924
  96.0 2.3 copy-start.4
  119.8 4.0 collective-permute-start.1
  123.9 1.2 copy-start.10
  127.8 195.3 %reduce-scatter.6.cloned.1.call-start = ((), (), s32[]{:S(2)}) async-start(), calls=%async_computation.12 | async-start | bytes 2228224 | tf_op jit(solution)/shard_map/reduce_scatter | solution.py:175
  131.3 2.2 collective-permute-start.2
  151.5 5.7 %copy-start.2 = (bf16[3,1280,2048]{2,1,0:T(8,128)(2,1)S(1)}, bf16[3,1280,2048]{2,1,0:T(8,128)(2,1)}, u32[]{:S(2)}) copy-start(bf16[3,1280,2048]{2,1,0:T(8,128)(2,1)} %pkv_ref.5) | copy-start | bytes 47185924
  157.2 2.4 copy-start.5
  179.7 4.9 %collective-permute-start.3 = (bf16[4,128,512]{2,1,0:T(8,128)(2,1)S(1)}, bf16[4,128,512]{2,1,0:T(8,128)(2,1)S(1)}, u32[]{:S(2)}, u32[]{:S(2)}) collective-permute-start(bf16[4,128,512]{2,1,0:T(8,128)(2,1)S(1)} %bitcast.97), channel_id=1, source_target_pairs={{0,16},{16,0},{1,17},{17,1},{2,18},{18,2},{3,19},{19,3},{4,20},{20... | collective-permute-start | bytes 1572872 | tf_op jit(solution)/shard_map/ppermute | solution.py:168
  187.6 212.3 %reduce-scatter.8.cloned.1.call-start = ((), (), s32[]{:S(2)}) async-start(), calls=%async_computation.14 | async-start | bytes 2228224 | tf_op jit(solution)/shard_map/reduce_scatter | solution.py:175
  191.1 2.2 collective-permute-start.4
  211.2 5.6 %copy-start.3 = (bf16[3,1280,2048]{2,1,0:T(8,128)(2,1)S(1)}, bf16[3,1280,2048]{2,1,0:T(8,128)(2,1)}, u32[]{:S(2)}) copy-start(bf16[3,1280,2048]{2,1,0:T(8,128)(2,1)} %pkv_ref.5) | copy-start | bytes 47185924
  216.8 2.3 copy-start.6
  241.2 4.0 collective-permute-start.5
Sparse Core Ops, SparseCore 0:
  10.7 47.4 all-gather.3
  60.4 49.0 all-gather.5
  111.6 48.8 all-gather.7
  163.6 81.1 reduce-scatter.3
  248.3 74.6 reduce-scatter.5
  326.1 73.6 reduce-scatter.7

commit v2 on v1

v2 whole, which is shorter than its diff:
```python
import functools

import jax
import jax.numpy as jnp
from jax import lax
from jax.experimental import pallas as pl
from jax.experimental.pallas import tpu as pltpu
from jax.sharding import Mesh
from jax.sharding import PartitionSpec as P

QUERY_HEADS = 64
KEY_HEADS = 8
HEAD_SIZE = 128
BEAMS_PER_PROMPT = 8
MASKED = -1e30


def rotary_tables(positions):
    half_dim = HEAD_SIZE // 2
    exponent = 2.0 * jnp.arange(half_dim, dtype=jnp.float32) / HEAD_SIZE
    frequency = jnp.exp(-jnp.log(jnp.float32(500000.0)) * exponent)
    angles = positions.astype(jnp.float32)[:, None] * frequency[None, :]
    cosine, sine = jnp.cos(angles), jnp.sin(angles)
    return (
        jnp.concatenate([cosine, cosine], axis=1)[:, None, :],
        jnp.concatenate([-sine, sine], axis=1)[:, None, :],
    )


def attend_kernel(
    parents_ref, lengths_ref, sources_ref, terms_ref, cos_ref, sin_ref, pkv_ref, bkv_ref,
    out_ref, fresh_ref, slab_ref,
):
    prompt = pl.program_id(0)
    beams, size = BEAMS_PER_PROMPT, HEAD_SIZE
    ratio = QUERY_HEADS // KEY_HEADS
    rows = beams * ratio
    context = pkv_ref.shape[1]
    past = bkv_ref.shape[0]
    generated = past // beams
    length = lengths_ref[prompt]
    cosine = jnp.broadcast_to(cos_ref[0], (beams, size))
    sine = jnp.broadcast_to(sin_ref[0], (beams, size))
    scale = size ** (-0.5) * 1.4426950408889634
    given = out_ref.shape[-1] // size
    slabs, _, columns = slab_ref.shape
    held = columns // size
    for n in range(slabs):
        slab_ref[n] = terms_ref[sources_ref[n], 0].astype(jnp.float32)

    def head(h):
        return slab_ref[h // held, :, (h % held) * size : (h % held + 1) * size]

    def rotated(v):
        v = v * cosine + pltpu.roll(v, size // 2, 1) * sine
        return v.astype(jnp.bfloat16).astype(jnp.float32)

    usable = lax.broadcasted_iota(jnp.int32, (2 * rows, context), 1) < length
    beam = lax.rem(lax.broadcasted_iota(jnp.int32, (2 * rows, past), 0), beams)
    first = jnp.zeros((2 * rows, past), jnp.int32)
    for b in range(beams):
        first = jnp.where(beam == b, parents_ref[prompt * beams + b] * generated, first)
    place = lax.broadcasted_iota(jnp.int32, (2 * rows, past), 1)
    chosen = (place >= first) & (place < first + generated)
    across = (((1,), (1,)), ((), ()))
    along = (((1,), (0,)), ((), ()))
    for j in range(KEY_HEADS // 2):
        ks = slice(2 * j * size, 2 * (j + 1) * size)
        vs = slice((KEY_HEADS + 2 * j) * size, (KEY_HEADS + 2 * j + 2) * size)
        queries, own_values, own_scores = [], [], []
        for g in (2 * j, 2 * j + 1):
            q = jnp.concatenate([rotated(head(g * ratio + r)) for r in range(ratio)], axis=0)
            own_key = rotated(head(QUERY_HEADS + g))
            own_value = head(QUERY_HEADS + KEY_HEADS + g)
            fresh_ref[0, :, g * size : (g + 1) * size] = own_key.astype(jnp.bfloat16)
            fresh_ref[0, :, (KEY_HEADS + g) * size : (KEY_HEADS + g + 1) * size] = own_value.astype(
                jnp.bfloat16
            )
            own_scores.append(
                jnp.sum(q * jnp.concatenate([own_key] * ratio, axis=0), axis=1, keepdims=True)
            )
            queries.append(q)
            own_values.append(jnp.concatenate([own_value] * ratio, axis=0))
        zero = jnp.zeros((rows, size), jnp.float32)
        q = jnp.concatenate(
            [
                jnp.concatenate([queries[0], zero], axis=1),
                jnp.concatenate([zero, queries[1]], axis=1),
            ],
            axis=0,
        ).astype(jnp.bfloat16)
        s1 = lax.dot_general(q, pkv_ref[0, :, ks], across, preferred_element_type=jnp.float32)
        s2 = lax.dot_general(q, bkv_ref[:, ks], across, preferred_element_type=jnp.float32)
        s3 = jnp.concatenate(own_scores, axis=0)
        s1 = jnp.where(usable, s1, MASKED)
        s2 = jnp.where(chosen, s2, MASKED)
        top = jnp.maximum(jnp.max(s1, axis=1, keepdims=True), jnp.max(s2, axis=1, keepdims=True))
        top = jnp.maximum(top, s3)
        e1 = jnp.exp2((s1 - top) * scale)
        e2 = jnp.exp2((s2 - top) * scale)
        e3 = jnp.exp2((s3 - top) * scale)
        total = jnp.sum(e1, axis=1, keepdims=True) + jnp.sum(e2, axis=1, keepdims=True) + e3
        o = lax.dot_general(
            e1.astype(jnp.bfloat16), pkv_ref[0, :, vs], along, preferred_element_type=jnp.float32
        )
        o = o + lax.dot_general(
            e2.astype(jnp.bfloat16), bkv_ref[:, vs], along, preferred_element_type=jnp.float32
        )
        for i in range(2):
            at = slice(i * rows, (i + 1) * rows)
            part = o[at, i * size : (i + 1) * size]
            part = (part + e3[at] * own_values[i]) / total[at]
            for r in range(ratio):
                h = (2 * j + i) * ratio + r
                lanes = slice((h % given) * size, (h % given + 1) * size)
                out_ref[h // given, 0, :, lanes] = part[r * beams : (r + 1) * beams].astype(
                    jnp.bfloat16
                )


def attend(terms, sources, cosine, sine, pkv, bkv, parents, lengths, groups):
    prompts, context, width = pkv.shape
    past = bkv.shape[0] // prompts
    count, _, beams, columns = terms.shape
    slabs = sources.shape[0]
    given = QUERY_HEADS * HEAD_SIZE // groups
    grid_spec = pltpu.PrefetchScalarGridSpec(
        num_scalar_prefetch=3,
        grid=(prompts,),
        in_specs=[
            pl.BlockSpec((count, 1, beams, columns), lambda i, *_: (0, i, 0, 0)),
            pl.BlockSpec((1, 1, HEAD_SIZE), lambda i, *_: (i, 0, 0)),
            pl.BlockSpec((1, 1, HEAD_SIZE), lambda i, *_: (i, 0, 0)),
            pl.BlockSpec((1, context, width), lambda i, *_: (i, 0, 0)),
            pl.BlockSpec((past, width), lambda i, *_: (i, 0)),
        ],
        out_specs=[
            pl.BlockSpec((groups, 1, beams, given), lambda i, *_: (0, i, 0, 0)),
            pl.BlockSpec((1, beams, width), lambda i, *_: (i, 0, 0)),
        ],
        scratch_shapes=[pltpu.VMEM((slabs, beams, columns), jnp.float32)],
    )
    return pl.pallas_call(
        attend_kernel,
        grid_spec=grid_spec,
        out_shape=[
            jax.ShapeDtypeStruct((groups, prompts, beams, given), jnp.bfloat16),
            jax.ShapeDtypeStruct((prompts, beams, width), jnp.bfloat16),
        ],
        compiler_params=pltpu.CompilerParams(vmem_limit_bytes=56 * 1024 * 1024),
        cost_estimate=pl.CostEstimate(
            flops=4 * prompts * 64 * HEAD_SIZE * KEY_HEADS * (context + past),
            bytes_accessed=2 * prompts * width * (context + past),
            transcendentals=prompts * 64 * KEY_HEADS * (context + past),
        ),
    )(parents, lengths, sources, terms, cosine, sine, pkv, bkv)


def project_kernel(which_ref, places_ref, *refs):
    *row_refs, own_ref, other_ref, out_ref, row_buffer, weight_buffer, row_sems, weight_sem = refs
    count, rows, depth = row_buffer.shape
    for which, ref in enumerate((own_ref, other_ref)):

        @pl.when(which_ref[0] == which)
        def _(ref=ref):
            pltpu.make_async_copy(ref, weight_buffer, weight_sem).start()

    copies, at = [], 0
    for s, ref in enumerate(row_refs):
        piece = row_buffer.at[at // rows, pl.ds(at % rows, ref.shape[0])]
        copies.append(pltpu.make_async_copy(ref, piece, row_sems.at[s]))
        copies[-1].start()
        at += ref.shape[0]
    pltpu.make_async_copy(own_ref, weight_buffer, weight_sem).wait()
    for copy in copies:
        copy.wait()
    product = jnp.dot(
        row_buffer[...].reshape(count * rows, depth),
        weight_buffer[...],
        preferred_element_type=jnp.float32,
    ).astype(jnp.bfloat16)
    for s in range(count):
        out_ref[places_ref[s]] = product[s * rows : (s + 1) * rows]


def project(which, places, gathered, own, other):
    rows, depth = gathered[0].shape
    count = sum(part.shape[0] for part in gathered) // rows
    columns = own.shape[1]
    scalars = pl.BlockSpec(memory_space=pltpu.SMEM)
    return pl.pallas_call(
        project_kernel,
        in_specs=[scalars, scalars]
        + [pl.BlockSpec(memory_space=pl.ANY)] * (len(gathered) + 2),
        out_specs=pl.BlockSpec(memory_space=pltpu.VMEM),
        out_shape=jax.ShapeDtypeStruct((count, rows, columns), jnp.bfloat16),
        scratch_shapes=[
            pltpu.VMEM((count, rows, depth), jnp.bfloat16),
            pltpu.VMEM((depth, columns), jnp.bfloat16),
            pltpu.SemaphoreType.DMA((len(gathered),)),
            pltpu.SemaphoreType.DMA,
        ],
        compiler_params=pltpu.CompilerParams(vmem_limit_bytes=56 * 1024 * 1024),
        cost_estimate=pl.CostEstimate(
            flops=2 * count * rows * depth * columns,
            bytes_accessed=2 * (count * rows * (depth + columns) + depth * columns),
            transcendentals=0,
        ),
    )(which.reshape(1), places, *gathered, own, other)


def output_kernel(core_ref, rows_ref, weight_ref, *refs):
    out_ref = refs[-1]
    xs, _, rows, _ = out_ref.shape
    product = jnp.dot(
        rows_ref[...], weight_ref[...], preferred_element_type=jnp.float32
    ).astype(jnp.bfloat16)
    for x in range(xs):
        out_ref[x, 0] = product[x * rows : (x + 1) * rows]


def output(core, value, weight, xs, buffer=None):
    rows, depth = value.shape
    columns = weight.shape[1]
    step = 256
    shape = (xs, 2, rows // xs, columns)
    grid_spec = pltpu.PrefetchScalarGridSpec(
        num_scalar_prefetch=1,
        grid=(columns // step,),
        in_specs=[
            pl.BlockSpec((rows, depth), lambda n, core: (0, 0)),
            pl.BlockSpec((depth, step), lambda n, core: (0, n)),
        ]
        + ([] if buffer is None else [pl.BlockSpec(memory_space=pl.ANY)]),
        out_specs=pl.BlockSpec((xs, 1, rows // xs, step), lambda n, core: (0, core[0], 0, n)),
    )
    return pl.pallas_call(
        output_kernel,
        grid_spec=grid_spec,
        out_shape=jax.ShapeDtypeStruct(shape, jnp.bfloat16),
        input_output_aliases={} if buffer is None else {3: 0},
        compiler_params=pltpu.CompilerParams(vmem_limit_bytes=32 * 1024 * 1024),
        cost_estimate=pl.CostEstimate(
            flops=2 * rows * depth * columns,
            bytes_accessed=2 * (rows * (depth + columns) + depth * columns),
            transcendentals=0,
        ),
    )(core.reshape(1), value, weight, *([] if buffer is None else [buffer]))


SWAP = [(0, 1), (1, 0)]


def shifted(value, axis, shift):
    size = lax.axis_size(axis)
    return lax.ppermute(value, axis, [(i, (i + shift) % size) for i in range(size)])


def beside(value, axis):
    return [value, shifted(value, axis, 1), shifted(value, axis, 3)]


def relayed(blocks, axis):
    value, near, back = blocks
    half = value.shape[0] // 2
    return [value, near, shifted(near[:half], axis, 1), shifted(back[half:], axis, 3), back]


def body(normed, qkv_weight, out_weight, prompt_key_value, beam_key_value, parents, lengths):
    prompts = prompt_key_value.shape[0]
    beams = BEAMS_PER_PROMPT
    nx, nz, ny = lax.axis_size("x"), lax.axis_size("z"), lax.axis_size("y")
    core = lax.axis_index("core")
    z, y = lax.axis_index("z"), lax.axis_index("y")
    depth, columns = qkv_weight.shape
    mine_rows = prompts * beams

    other = lax.ppermute(qkv_weight, "y", [(i, ny - 1 - i) for i in range(ny)])
    own = beside(normed, "z")
    swapped = lax.ppermute(normed, "y", [(i, i ^ 1) for i in range(ny)])
    *own, swapped = lax.optimization_barrier((*own, swapped))
    swapped = beside(swapped, "z")
    own = relayed(own, "z")
    swapped = relayed(swapped, "z")
    out_weight, other = lax.optimization_barrier((out_weight, other))
    weight = lax.all_gather(out_weight, "y", axis=0, tiled=True)

    cosine, sine = rotary_tables(lengths + beam_key_value.shape[1])
    history = beam_key_value.reshape(-1, beam_key_value.shape[-1])
    slab = jnp.arange(nz * ny, dtype=jnp.int32)
    slab_z, slab_y = slab // ny, slab % ny
    slots = jnp.where(slab_y // 2 == core, 0, 1)
    sender_y = jnp.where(slots == 0, slab_y, ny - 1 - slab_y)
    sources = (jnp.where(slots == core, 0, nz) + slab_z) * 2 + sender_y % 2
    sources = sources.astype(jnp.int32)
    from_z = (z - jnp.arange(nz, dtype=jnp.int32)) % nz
    places = jnp.concatenate([from_z * 2 + y % 2, from_z * 2 + 1 - y % 2]).astype(jnp.int32)
    core = core.astype(jnp.int32)

    gathered = own + swapped
    away = project(1 - core, places, gathered, qkv_weight, other)
    arrived = lax.ppermute(away, "core", SWAP)
    mine = project(core, places, gathered, qkv_weight, other)
    terms = (mine.astype(jnp.float32) + arrived.astype(jnp.float32)).astype(jnp.bfloat16)
    terms = terms.reshape(nx * nz * ny, mine_rows, columns)
    terms = lax.all_to_all(terms, ("x", "z", "y"), split_axis=0, concat_axis=0, tiled=True)
    terms = jnp.sum(terms.reshape(nx, nz, 2, 2, mine_rows, columns).astype(jnp.float32), axis=0)
    terms = terms.astype(jnp.bfloat16)
    kept = lax.dynamic_index_in_dim(terms, core, 1, keepdims=False)
    passed = lax.dynamic_index_in_dim(terms, 1 - core, 1, keepdims=False)
    terms = jnp.stack([kept, lax.ppermute(passed, "core", SWAP)])
    terms = terms.reshape(4 * nz, prompts, beams, columns)
    out, fresh = attend(
        terms, sources, cosine, sine, prompt_key_value, history, parents, lengths, nz
    )
    out = out.reshape(nz, mine_rows, -1)
    copies = jnp.broadcast_to(out[None], (nx,) + out.shape).reshape((nx * nz,) + out.shape[1:])
    mine = lax.all_to_all(copies, ("x", "z"), split_axis=0, concat_axis=0, tiled=True)
    mine = mine.reshape(nx * nz * mine_rows, -1)
    twin = lax.ppermute(mine, "core", SWAP)
    product = output(core, mine, weight, nx)
    product = output(1 - core, twin, weight, nx, product)
    product = product.reshape(nz * ny, 2 * mine_rows, -1)
    terms = lax.all_to_all(product, ("z", "y"), split_axis=0, concat_axis=0, tiled=True)
    terms = terms.reshape(nz, ny, 2, mine_rows, -1).astype(jnp.float32)
    result = jnp.sum(terms, axis=0).astype(jnp.bfloat16).transpose(1, 0, 2, 3)
    return (result.reshape(-1, result.shape[-1]), fresh.reshape(mine_rows, -1))


def solution(mesh):
    chips = Mesh(mesh.devices.reshape(4, 2, 4, 4), ("x", "core", "z", "y"))
    gx, gy = ("x", "core"), ("z", "y")
    whole = gx + gy
    return jax.shard_map(
        body,
        mesh=chips,
        in_specs=(
            P(gy, gx),
            P(gx, gy),
            P(gy, gx),
            P(whole, None, None),
            P(whole, None, None),
            P(whole),
            P(whole),
        ),
        out_specs=(P(gy, gx), P(whole, None)),
        check_vma=False,
    )
```

time: 410 us -> 196 us (0.48)
  waiting for transfers between devices: 223 us -> 48 us
  blocking collectives: 85.7 us -> 55.5 us
  local copies, waits for them, and re-layouts: 29.5 us -> 6.14 us
  Pallas kernels: 13.6 us -> 33.3 us
  matrix products: 18 us -> 0 us
  starting transfers between devices: 19.3 us -> 31.9 us
    reduce_scatter x3 -> x0, waiting for transfers between devices: 151 us -> none  [body(): lax.psum_scatter(product, ('z', 'y'), scatter_dimension=0, tiled=True)]
    all_gather x3 -> x1, waiting for transfers between devices: 47.6 us -> 0.01 us  [body(): weight = lax.all_gather(out_weight, 'y', axis=0, tiled=True)]
    all_to_all x5 -> x2, blocking collectives: 85.7 us -> 55.5 us  [the longest x1 30.2 us: body(): lax.all_to_all(copies, ('x', 'z'), split_axis=0, concat_axis=0, tiled=True)]
    unnamed x22 -> x26, local copies, waits for them, and re-layouts: 26.4 us -> 2.91 us
    pallas_call x3 -> x5, Pallas kernels: 13.6 us -> 33.3 us  [the longest x2 14 us: project(): pl.pallas_call(project_kernel, in_specs=[scalars, scalars] + [pl.BlockSpe...]
    dot_general x6 -> x0, matrix products: 18 us -> none  [the longest x3 10.2 us: body(): terms = jnp.dot(rows, qkv_weight, preferred_element_type=jnp.float32)]
    all_to_all x1, waiting for transfers between devices: 13 us -> 29.3 us  [body(): lax.all_to_all(terms, ('x', 'z', 'y'), split_axis=0, concat_axis=0, tiled...]
    ppermute x6 -> x13, starting transfers between devices: 11.1 us -> 24 us  [the longest x8 12 us: shifted(): lax.ppermute(value, axis, [(i, (i + shift) % size) for i in range(size)])]
  transfers between devices with their start and end apart: 13 -> 15, of which waited for: 10 -> 6; matrix products, arithmetic and copies ran while one was open for 6% -> 4% of each run, Pallas kernels for 3% -> 12%
where the time goes in v2:
time: 196 us
  blocking collectives  55.5 us (28%)
  waiting for transfers between devices  48 us (24%)
  Pallas kernels  33.3 us (17%)
  starting transfers between devices  31.9 us (16%)
  between operations  14.3 us (7%)
  other arithmetic  6.63 us (3%)
  local copies, waits for them, and re-layouts  6.14 us (3%)
    all_to_all x1, blocking collectives, body(): lax.all_to_all(copies, ('x', 'z'), split_axis=0, concat_axis=0, tiled=True)  30.2 us
    all_to_all x1, waiting for transfers between devices, body(): lax.all_to_all(terms, ('x', 'z', 'y'), split_axis=0, concat_axis=0, tiled...  29.3 us
    all_to_all x1, blocking collectives, body(): lax.all_to_all(product, ('z', 'y'), split_axis=0, concat_axis=0, tiled=True)  25.4 us
    ppermute x8, waiting for transfers between devices, shifted(): lax.ppermute(value, axis, [(i, (i + shift) % size) for i in range(size)])  15.7 us
    pallas_call x2, Pallas kernels, project(): pl.pallas_call(project_kernel, in_specs=[scalars, scalars] + [pl.BlockSpe...  14 us
    pallas_call x1, Pallas kernels, attend(): pl.pallas_call(attend_kernel, grid_spec=grid_spec, out_shape=[jax.ShapeDt...  13.3 us
    ppermute x8, starting transfers between devices, shifted(): lax.ppermute(value, axis, [(i, (i + shift) % size) for i in range(size)])  12 us
    all_to_all x1, starting transfers between devices, body(): lax.all_to_all(terms, ('x', 'z', 'y'), split_axis=0, concat_axis=0, tiled...  7.84 us
  transfers between devices with their start and end apart: 15, of which 6 were waited for; matrix products, arithmetic and copies ran while one was open for 4% of the time, Pallas kernels for 12%

profile of v2, /device:TPU:1, one launch (start us, length us, event | category | flops | bytes accessed | tf_op | source)
XLA Modules:
  0.0 195.7 jit_solution(4194970939220559449)
XLA Ops:
  7.2 3.6 %collective-permute-start.9 = (bf16[1024,640]{1,0:T(8,128)(2,1)}, bf16[1024,640]{1,0:T(8,128)(2,1)S(1)}, u32[]{:S(2)}, u32[]{:S(2)}) collective-permute-start(bf16[1024,640]{1,0:T(8,128)(2,1)} %refs_10_.3), channel_id=1, source_target_pairs={{0,3},{1,2},{2,1},{3,0},{4,7},{5,6},{6,5},{7,4},{8,11},{9,10},{10,... | collective-permute-start | bytes 3932168 | tf_op jit(solution)/shard_map/ppermute | solution.py:278
  10.9 1.6 collective-permute-start
  12.5 2.1 %collective-permute-start.1 = (bf16[192,1024]{1,0:T(8,128)(2,1)}, bf16[192,1024]{1,0:T(8,128)(2,1)S(1)}, u32[]{:S(2)}, u32[]{:S(2)}) collective-permute-start(bf16[192,1024]{1,0:T(8,128)(2,1)} %refs_0_.1), channel_id=1, source_target_pairs={{0,12},{4,0},{8,4},{12,8},{1,13},{5,1},{9,5},{13,9},{2,14},{6,2},{... | collective-permute-start | bytes 1179656 | tf_op jit(solution)/shard_map/ppermute | solution.py:256
  14.6 8.7 %collective-permute-done.refs_1_ = bf16[192,1024]{1,0:T(8,128)(2,1)S(1)} collective-permute-done((bf16[192,1024]{1,0:T(8,128)(2,1)}, bf16[192,1024]{1,0:T(8,128)(2,1)S(1)}, u32[]{:S(2)}, u32[]{:S(2)}) %collective-permute-start) | collective-permute-done | bytes 393248 | tf_op jit(solution)/shard_map/ppermute | solution.py:256
  23.3 0.8 collective-permute-done.2.refs_5_
  24.2 2.7 %collective-permute-start.7 = (bf16[192,1024]{1,0:T(8,128)(2,1)S(1)}, bf16[192,1024]{1,0:T(8,128)(2,1)S(1)}, u32[]{:S(2)}, u32[]{:S(2)}) collective-permute-start(bf16[192,1024]{1,0:T(8,128)(2,1)S(1)} %collective-permute-done.2.refs_5_), channel_id=1, source_target_pairs={{0,12},{4,0},{8,4},{12,8},{1,13},{5,1},{9,5},{13,9},{2,14},{6,2},{... | collective-permute-start | bytes 1179656 | tf_op jit(solution)/shard_map/ppermute | solution.py:256
  27.0 2.7 %collective-permute-start.4 = (bf16[96,1024]{1,0:T(8,128)(2,1)S(1)}, bf16[96,1024]{1,0:T(8,128)(2,1)S(1)}, u32[]{:S(2)}, u32[]{:S(2)}) collective-permute-start(bf16[96,1024]{1,0:T(8,128)(2,1)S(1)} %slice.13), channel_id=1, source_target_pairs={{0,12},{4,0},{8,4},{12,8},{1,13},{5,1},{9,5},{13,9},{2,14},{6,2},{... | collective-permute-start | bytes 589832 | tf_op jit(solution)/shard_map/ppermute | solution.py:256
  29.7 4.1 %collective-permute-done.5.refs_6_ = bf16[192,1024]{1,0:T(8,128)(2,1)S(1)} collective-permute-done((bf16[192,1024]{1,0:T(8,128)(2,1)S(1)}, bf16[192,1024]{1,0:T(8,128)(2,1)S(1)}, u32[]{:S(2)}, u32[]{:S(2)}) %collective-permute-start.5) | collective-permute-done | bytes 393248 | tf_op jit(solution)/shard_map/ppermute | solution.py:256
  34.0 2.7 %collective-permute-start.8 = (bf16[96,1024]{1,0:T(8,128)(2,1)S(1)}, bf16[96,1024]{1,0:T(8,128)(2,1)S(1)}, u32[]{:S(2)}, u32[]{:S(2)}) collective-permute-start(bf16[96,1024]{1,0:T(8,128)(2,1)S(1)} %slice.17), channel_id=1, source_target_pairs={{0,12},{4,0},{8,4},{12,8},{1,13},{5,1},{9,5},{13,9},{2,14},{6,2},{... | collective-permute-start | bytes 589832 | tf_op jit(solution)/shard_map/ppermute | solution.py:256
  36.7 0.6 pad_add_fusion.places_ref
  37.3 2.1 %collective-permute-done.9.refs_11_ = bf16[1024,640]{1,0:T(8,128)(2,1)S(1)} collective-permute-done((bf16[1024,640]{1,0:T(8,128)(2,1)}, bf16[1024,640]{1,0:T(8,128)(2,1)S(1)}, u32[]{:S(2)}, u32[]{:S(2)}) %collective-permute-start.9) | collective-permute-done | bytes 1310752 | tf_op jit(solution)/shard_map/ppermute | solution.py:278
  39.4 2.8 %collective-permute-done.6.refs_7_ = bf16[96,1024]{1,0:T(8,128)(2,1)S(1)} collective-permute-done((bf16[96,1024]{1,0:T(8,128)(2,1)S(1)}, bf16[96,1024]{1,0:T(8,128)(2,1)S(1)}, u32[]{:S(2)}, u32[]{:S(2)}) %collective-permute-start.6) | collective-permute-done | bytes 196640 | tf_op jit(solution)/shard_map/ppermute | solution.py:256
  42.4 0.6 copy-done.10
  43.0 7.0 %shard_map.87 = bf16[8,192,640]{2,1,0:T(8,128)(2,1)} custom-call(s32[1]{0:T(128)} %bitcast.which_ref.core_ref, s32[8]{0:T(128)} %pad_add_fusion.places_ref, bf16[192,1024]{1,0:T(8,128)(2,1)} %refs_0_.1, bf16[192,1024]{1,0:T(8,128)(2,1)} %copy-done.3, bf16[96,1024]{1,0:T(8,128)(2,1)} %copy-done.8, bf16[96,1024]{1,0:T(8,128)(2,1)} %copy-done.9, ...), custom_call_target="tpu_custom_call" | custom-call | flops 2013265920 | bytes 6422528 | tf_op jit(solution)/shard_map/pallas_call | solution.py:191
  50.1 4.4 %collective-permute-start.10 = (bf16[8,192,640]{2,1,0:T(8,128)(2,1)}, bf16[8,192,640]{2,1,0:T(8,128)(2,1)S(1)}, u32[]{:S(2)}, u32[]{:S(2)}) collective-permute-start(bf16[8,192,640]{2,1,0:T(8,128)(2,1)} %shard_map.87), channel_id=1, source_target_pairs={{0,16},{16,0},{1,17},{17,1},{2,18},{18,2},{3,19},{19,3},{4,20},{20... | collective-permute-start | bytes 5898248 | tf_op jit(solution)/shard_map/ppermute | solution.py:302
  54.5 7.0 %shard_map.86 = bf16[8,192,640]{2,1,0:T(8,128)(2,1)} custom-call(s32[1]{0:T(128)} %bitcast.1.which_ref.core_ref, s32[8]{0:T(128)} %pad_add_fusion.places_ref, bf16[192,1024]{1,0:T(8,128)(2,1)} %refs_0_.1, bf16[192,1024]{1,0:T(8,128)(2,1)} %copy-done.3, bf16[96,1024]{1,0:T(8,128)(2,1)} %copy-done.8, bf16[96,1024]{1,0:T(8,128)(2,1)} %copy-done.9, ...), custom_call_target="tpu_custom_call" | custom-call | flops 2013265920 | bytes 6422528 | tf_op jit(solution)/shard_map/pallas_call | solution.py:191
  61.5 3.5 %add_convert_fusion = bf16[8,192,640]{2,1,0:T(8,128)(2,1)} fusion(bf16[8,192,640]{2,1,0:T(8,128)(2,1)S(1)} %collective-permute-done.10, bf16[8,192,640]{2,1,0:T(8,128)(2,1)} %shard_map.86), kind=kLoop, calls=%fused_computation | loop fusion | flops 3932160 | bytes 5898240 | tf_op jit(solution)/shard_map/convert_element_type | solution.py:304
  65.0 7.8 %all-to-all-start = ((bf16[64,24,640]{2,1,0:T(8,128)(2,1)}), bf16[64,24,640]{2,1,0:T(8,128)(2,1)S(1)}, u32[]{:S(2)}, u32[]{:S(2)}) async-start(bf16[64,24,640]{2,1,0:T(8,128)(2,1)} %bitcast.25), calls=%async_computation | async-start | bytes 3932160 | tf_op jit(solution)/shard_map/all_to_all | solution.py:306
  73.0 29.3 %all-to-all-done = bf16[64,24,640]{2,1,0:T(8,128)(2,1)S(1)} async-done(((bf16[64,24,640]{2,1,0:T(8,128)(2,1)}), bf16[64,24,640]{2,1,0:T(8,128)(2,1)S(1)}, u32[]{:S(2)}, u32[]{:S(2)}) %all-to-all-start) | async-done | bytes 1966112 | tf_op jit(solution)/shard_map/all_to_all | solution.py:306
  102.9 1.6 collective-permute-start.11
  104.6 0.6 copy.12.cos_ref
  105.2 0.6 broadcast_in_dim.22.sin_ref
  106.4 0.8 pad_maximum_fusion
  107.2 13.3 %shard_map.88 = (bf16[4,3,8,2048]{3,2,1,0:T(8,128)(2,1)}, bf16[3,8,2048]{2,1,0:T(8,128)(2,1)}) custom-call(s32[24]{0:T(128)} %parents_ref.1, s32[3]{0:T(128)} %lengths_ref.1, s32[16]{0:T(128)} %fusion.sources_ref, bf16[16,3,8,640]{3,2,1,0:T(8,128)(2,1)} %bitcast.29, f32[3,1,128]{2,1,0:T(1,128)} %copy.12.cos_ref, f32[3,1,128]{2,1,0:T(1,128)} %broadcast_in_dim.22.sin_ref, ...), custom_call_target="tpu_custom_call" | custom-call | flops 1308622848 | bytes 20447232 | tf_op jit(solution)/shard_map/pallas_call | solution.py:143
  120.6 1.2 broadcast_in_dim.24
  121.8 30.2 %all_to_all.15 = bf16[16,24,2048]{2,1,0:T(8,128)(2,1)S(1)} all-to-all(bf16[16,24,2048]{2,1,0:T(8,128)(2,1)S(1)} %bitcast.27), channel_id=1, replica_groups=mesh['x'=4,'core'=2,'z'=4,'y'=4] {'x','z'}, dimensions={0} | all-to-all | bytes 3145728 | tf_op jit(solution)/shard_map/all_to_all | solution.py:318
  151.9 2.3 %collective-permute-start.12 = (bf16[384,2048]{1,0:T(8,128)(2,1)S(1)}, bf16[384,2048]{1,0:T(8,128)(2,1)S(1)}, u32[]{:S(2)}, u32[]{:S(2)}) collective-permute-start(bf16[384,2048]{1,0:T(8,128)(2,1)S(1)} %bitcast.22), channel_id=1, source_target_pairs={{0,16},{16,0},{1,17},{17,1},{2,18},{18,2},{3,19},{19,3},{4,20},{20... | collective-permute-start | bytes 4718600 | tf_op jit(solution)/shard_map/ppermute | solution.py:320
  154.2 2.2 %copy-done = bf16[2048,1024]{1,0:T(8,128)(2,1)S(1)} copy-done((bf16[2048,1024]{1,0:T(8,128)(2,1)S(1)}, bf16[2048,1024]{1,0:T(8,128)(2,1)}, u32[]{:S(2)}) %copy-start) | copy-done | bytes 4194328
  156.4 3.0 %shard_map.89.refs_0_ = bf16[4,2,96,1024]{3,2,1,0:T(8,128)(2,1)S(1)} custom-call(s32[1]{0:T(128)} %bitcast.1.which_ref.core_ref, bf16[384,2048]{1,0:T(8,128)(2,1)S(1)} %bitcast.23, bf16[2048,1024]{1,0:T(8,128)(2,1)S(1)} %copy-done), custom_call_target="tpu_custom_call" | custom-call | flops 1610612736 | bytes 6553600 | tf_op jit(solution)/shard_map/pallas_call | solution.py:237
  159.4 3.0 %shard_map.90 = bf16[4,2,96,1024]{3,2,1,0:T(8,128)(2,1)S(1)} custom-call(s32[1]{0:T(128)} %bitcast.which_ref.core_ref, bf16[384,2048]{1,0:T(8,128)(2,1)S(1)} %collective-permute-done.12.rows_ref, bf16[2048,1024]{1,0:T(8,128)(2,1)S(1)} %copy-done.1, bf16[4,2,96,1024]{3,2,1,0:T(8,128)(2,1)S(1)} %shard_map.89.refs_0_), custom_call_target="tpu_custom_call", output_to_operand_aliasing={{}: (3, {})} | custom-call | flops 1610612736 | bytes 6553600 | tf_op jit(solution)/shard_map/pallas_call | solution.py:237
  162.4 25.4 %all_to_all.16 = bf16[16,48,1024]{2,1,0:T(8,128)(2,1)S(1)} all-to-all(bf16[16,48,1024]{2,1,0:T(8,128)(2,1)S(1)} %bitcast.21), channel_id=1, replica_groups=mesh['x'=4,'core'=2,'z'=4,'y'=4] {'z','y'}, dimensions={0} | all-to-all | bytes 3145728 | tf_op jit(solution)/shard_map/all_to_all | solution.py:324
  188.1 0.8 copy.13
  (53 shorter events, 2.2 us)
Async XLA Ops:
  7.2 147.1 %all-gather.2.cloned.1.call-start = ((), (), s32[]{:S(2)}) async-start(), calls=%async_computation.3 | async-start | bytes 5242880 | tf_op jit(solution)/shard_map/all_gather | solution.py:286
  7.2 32.2 %collective-permute-start.9 = (bf16[1024,640]{1,0:T(8,128)(2,1)}, bf16[1024,640]{1,0:T(8,128)(2,1)S(1)}, u32[]{:S(2)}, u32[]{:S(2)}) collective-permute-start(bf16[1024,640]{1,0:T(8,128)(2,1)} %refs_10_.3), channel_id=1, source_target_pairs={{0,3},{1,2},{2,1},{3,0},{4,7},{5,6},{6,5},{7,4},{8,11},{9,10},{10,... | collective-permute-start | bytes 3932168 | tf_op jit(solution)/shard_map/ppermute | solution.py:278
  10.9 12.5 %collective-permute-start = (bf16[192,1024]{1,0:T(8,128)(2,1)}, bf16[192,1024]{1,0:T(8,128)(2,1)S(1)}, u32[]{:S(2)}, u32[]{:S(2)}) collective-permute-start(bf16[192,1024]{1,0:T(8,128)(2,1)} %refs_0_.1), channel_id=1, source_target_pairs={{0,4},{4,8},{8,12},{12,0},{1,5},{5,9},{9,13},{13,1},{2,6},{6,10},{... | collective-permute-start | bytes 1179656 | tf_op jit(solution)/shard_map/ppermute | solution.py:256
  12.5 10.9 %collective-permute-start.1 = (bf16[192,1024]{1,0:T(8,128)(2,1)}, bf16[192,1024]{1,0:T(8,128)(2,1)S(1)}, u32[]{:S(2)}, u32[]{:S(2)}) collective-permute-start(bf16[192,1024]{1,0:T(8,128)(2,1)} %refs_0_.1), channel_id=1, source_target_pairs={{0,12},{4,0},{8,4},{12,8},{1,13},{5,1},{9,5},{13,9},{2,14},{6,2},{... | collective-permute-start | bytes 1179656 | tf_op jit(solution)/shard_map/ppermute | solution.py:256
  14.6 9.6 %collective-permute-start.2 = (bf16[192,1024]{1,0:T(8,128)(2,1)}, bf16[192,1024]{1,0:T(8,128)(2,1)S(1)}, u32[]{:S(2)}, u32[]{:S(2)}) collective-permute-start(bf16[192,1024]{1,0:T(8,128)(2,1)} %refs_0_.1), channel_id=1, source_target_pairs={{0,1},{1,0},{2,3},{3,2},{4,5},{5,4},{6,7},{7,6},{8,9},{9,8},{10,11... | collective-permute-start | bytes 1179656 | tf_op jit(solution)/shard_map/ppermute | solution.py:280
  23.3 18.9 %copy-start.3 = (bf16[192,1024]{1,0:T(8,128)(2,1)}, bf16[192,1024]{1,0:T(8,128)(2,1)S(1)}, u32[]{:S(2)}) copy-start(bf16[192,1024]{1,0:T(8,128)(2,1)S(1)} %collective-permute-done.refs_1_) | copy-start | bytes 1179652
  23.3 18.9 %copy-start.4 = (bf16[192,1024]{1,0:T(8,128)(2,1)}, bf16[192,1024]{1,0:T(8,128)(2,1)S(1)}, u32[]{:S(2)}) copy-start(bf16[192,1024]{1,0:T(8,128)(2,1)S(1)} %collective-permute-done.1.refs_4_) | copy-start | bytes 1179652
  24.2 18.1 %copy-start.7 = (bf16[192,1024]{1,0:T(8,128)(2,1)}, bf16[192,1024]{1,0:T(8,128)(2,1)S(1)}, u32[]{:S(2)}) copy-start(bf16[192,1024]{1,0:T(8,128)(2,1)S(1)} %collective-permute-done.2.refs_5_) | copy-start | bytes 1179652
  24.2 9.7 %collective-permute-start.5 = (bf16[192,1024]{1,0:T(8,128)(2,1)S(1)}, bf16[192,1024]{1,0:T(8,128)(2,1)S(1)}, u32[]{:S(2)}, u32[]{:S(2)}) collective-permute-start(bf16[192,1024]{1,0:T(8,128)(2,1)S(1)} %collective-permute-done.2.refs_5_), channel_id=1, source_target_pairs={{0,4},{4,8},{8,12},{12,0},{1,5},{5,9},{9,13},{13,1},{2,6},{6,10},{... | collective-permute-start | bytes 1179656 | tf_op jit(solution)/shard_map/ppermute | solution.py:256
  24.2 9.8 %collective-permute-start.7 = (bf16[192,1024]{1,0:T(8,128)(2,1)S(1)}, bf16[192,1024]{1,0:T(8,128)(2,1)S(1)}, u32[]{:S(2)}, u32[]{:S(2)}) collective-permute-start(bf16[192,1024]{1,0:T(8,128)(2,1)S(1)} %collective-permute-done.2.refs_5_), channel_id=1, source_target_pairs={{0,12},{4,0},{8,4},{12,8},{1,13},{5,1},{9,5},{13,9},{2,14},{6,2},{... | collective-permute-start | bytes 1179656 | tf_op jit(solution)/shard_map/ppermute | solution.py:256
  26.9 12.5 %collective-permute-start.3 = (bf16[96,1024]{1,0:T(8,128)(2,1)S(1)}, bf16[96,1024]{1,0:T(8,128)(2,1)S(1)}, u32[]{:S(2)}, u32[]{:S(2)}) collective-permute-start(bf16[96,1024]{1,0:T(8,128)(2,1)S(1)} %slice.12), channel_id=1, source_target_pairs={{0,4},{4,8},{8,12},{12,0},{1,5},{5,9},{9,13},{13,1},{2,6},{6,10},{... | collective-permute-start | bytes 589832 | tf_op jit(solution)/shard_map/ppermute | solution.py:256
  27.0 12.4 %collective-permute-start.4 = (bf16[96,1024]{1,0:T(8,128)(2,1)S(1)}, bf16[96,1024]{1,0:T(8,128)(2,1)S(1)}, u32[]{:S(2)}, u32[]{:S(2)}) collective-permute-start(bf16[96,1024]{1,0:T(8,128)(2,1)S(1)} %slice.13), channel_id=1, source_target_pairs={{0,12},{4,0},{8,4},{12,8},{1,13},{5,1},{9,5},{13,9},{2,14},{6,2},{... | collective-permute-start | bytes 589832 | tf_op jit(solution)/shard_map/ppermute | solution.py:256
  33.9 8.5 %copy-start.5 = (bf16[192,1024]{1,0:T(8,128)(2,1)}, bf16[192,1024]{1,0:T(8,128)(2,1)S(1)}, u32[]{:S(2)}) copy-start(bf16[192,1024]{1,0:T(8,128)(2,1)S(1)} %collective-permute-done.5.refs_6_) | copy-start | bytes 1179652
  33.9 8.4 %collective-permute-start.6 = (bf16[96,1024]{1,0:T(8,128)(2,1)S(1)}, bf16[96,1024]{1,0:T(8,128)(2,1)S(1)}, u32[]{:S(2)}, u32[]{:S(2)}) collective-permute-start(bf16[96,1024]{1,0:T(8,128)(2,1)S(1)} %slice.16), channel_id=1, source_target_pairs={{0,4},{4,8},{8,12},{12,0},{1,5},{5,9},{9,13},{13,1},{2,6},{6,10},{... | collective-permute-start | bytes 589832 | tf_op jit(solution)/shard_map/ppermute | solution.py:256
  34.0 8.4 %copy-start.6 = (bf16[192,1024]{1,0:T(8,128)(2,1)}, bf16[192,1024]{1,0:T(8,128)(2,1)S(1)}, u32[]{:S(2)}) copy-start(bf16[192,1024]{1,0:T(8,128)(2,1)S(1)} %collective-permute-done.7.refs_9_) | copy-start | bytes 1179652
  34.0 8.3 %collective-permute-start.8 = (bf16[96,1024]{1,0:T(8,128)(2,1)S(1)}, bf16[96,1024]{1,0:T(8,128)(2,1)S(1)}, u32[]{:S(2)}, u32[]{:S(2)}) collective-permute-start(bf16[96,1024]{1,0:T(8,128)(2,1)S(1)} %slice.17), channel_id=1, source_target_pairs={{0,12},{4,0},{8,4},{12,8},{1,13},{5,1},{9,5},{13,9},{2,14},{6,2},{... | collective-permute-start | bytes 589832 | tf_op jit(solution)/shard_map/ppermute | solution.py:256
  39.4 2.9 %copy-start.2 = (bf16[1024,640]{1,0:T(8,128)(2,1)}, bf16[1024,640]{1,0:T(8,128)(2,1)S(1)}, u32[]{:S(2)}) copy-start(bf16[1024,640]{1,0:T(8,128)(2,1)S(1)} %collective-permute-done.9.refs_11_) | copy-start | bytes 3932164
  39.4 2.9 %copy-start.8 = (bf16[96,1024]{1,0:T(8,128)(2,1)}, bf16[96,1024]{1,0:T(8,128)(2,1)S(1)}, u32[]{:S(2)}) copy-start(bf16[96,1024]{1,0:T(8,128)(2,1)S(1)} %collective-permute-done.3.refs_2_) | copy-start | bytes 589828
  39.4 2.9 %copy-start.9 = (bf16[96,1024]{1,0:T(8,128)(2,1)}, bf16[96,1024]{1,0:T(8,128)(2,1)S(1)}, u32[]{:S(2)}) copy-start(bf16[96,1024]{1,0:T(8,128)(2,1)S(1)} %collective-permute-done.4.refs_3_) | copy-start | bytes 589828
  42.3 0.7 copy-start.10
  42.3 0.8 copy-start.11
  50.1 11.4 %collective-permute-start.10 = (bf16[8,192,640]{2,1,0:T(8,128)(2,1)}, bf16[8,192,640]{2,1,0:T(8,128)(2,1)S(1)}, u32[]{:S(2)}, u32[]{:S(2)}) collective-permute-start(bf16[8,192,640]{2,1,0:T(8,128)(2,1)} %shard_map.87), channel_id=1, source_target_pairs={{0,16},{16,0},{1,17},{17,1},{2,18},{18,2},{3,19},{19,3},{4,20},{20... | collective-permute-start | bytes 5898248 | tf_op jit(solution)/shard_map/ppermute | solution.py:302
  65.0 7.9 %copy-start.12 = (s32[3]{0:T(128)S(1)}, s32[3]{0:T(128)}, u32[]{:S(2)}) copy-start(s32[3]{0:T(128)} %lengths_ref.1) | copy-start | bytes 40
  65.0 37.3 %all-to-all-start = ((bf16[64,24,640]{2,1,0:T(8,128)(2,1)}), bf16[64,24,640]{2,1,0:T(8,128)(2,1)S(1)}, u32[]{:S(2)}, u32[]{:S(2)}) async-start(bf16[64,24,640]{2,1,0:T(8,128)(2,1)} %bitcast.25), calls=%async_computation | async-start | bytes 3932160 | tf_op jit(solution)/shard_map/all_to_all | solution.py:306
  102.9 3.5 %collective-permute-start.11 = (bf16[4,2,24,640]{3,2,1,0:T(8,128)(2,1)S(1)}, bf16[4,2,24,640]{3,2,1,0:T(8,128)(2,1)S(1)}, u32[]{:S(2)}, u32[]{:S(2)}) collective-permute-start(bf16[4,2,24,640]{3,2,1,0:T(8,128)(2,1)S(1)} %get-tuple-element.19), channel_id=1, source_target_pairs={{0,16},{16,0},{1,17},{17,1},{2,18},{18,2},{3,19},{19,3},{4,20},{20... | collective-permute-start | bytes 737288 | tf_op jit(solution)/shard_map/ppermute | solution.py:311
  151.9 7.5 %collective-permute-start.12 = (bf16[384,2048]{1,0:T(8,128)(2,1)S(1)}, bf16[384,2048]{1,0:T(8,128)(2,1)S(1)}, u32[]{:S(2)}, u32[]{:S(2)}) collective-permute-start(bf16[384,2048]{1,0:T(8,128)(2,1)S(1)} %bitcast.22), channel_id=1, source_target_pairs={{0,16},{16,0},{1,17},{17,1},{2,18},{18,2},{3,19},{19,3},{4,20},{20... | collective-permute-start | bytes 4718600 | tf_op jit(solution)/shard_map/ppermute | solution.py:320
  154.2 2.2 %copy-start = (bf16[2048,1024]{1,0:T(8,128)(2,1)S(1)}, bf16[2048,1024]{1,0:T(8,128)(2,1)}, u32[]{:S(2)}) copy-start(bf16[2048,1024]{1,0:T(8,128)(2,1)} %all-gather.2.cloned.1.call-done.weight_ref) | copy-start | bytes 12582916
  156.4 3.0 %copy-start.1 = (bf16[2048,1024]{1,0:T(8,128)(2,1)S(1)}, bf16[2048,1024]{1,0:T(8,128)(2,1)}, u32[]{:S(2)}) copy-start(bf16[2048,1024]{1,0:T(8,128)(2,1)} %all-gather.2.cloned.1.call-done.weight_ref) | copy-start | bytes 12582916
Sparse Core Ops, SparseCore 0:
  54.6 67.8 all-gather.1

commit v3 on v2

--- a/solution.py
+++ b/solution.py
@@ -109,16 +109,15 @@
         for i in range(2):
             at = slice(i * rows, (i + 1) * rows)
             part = o[at, i * size : (i + 1) * size]
-            part = (part + e3[at] * own_values[i]) / total[at]
+            part = ((part + e3[at] * own_values[i]) / total[at]).astype(jnp.bfloat16)
             for r in range(ratio):
                 h = (2 * j + i) * ratio + r
                 lanes = slice((h % given) * size, (h % given + 1) * size)
-                out_ref[h // given, 0, :, lanes] = part[r * beams : (r + 1) * beams].astype(
-                    jnp.bfloat16
-                )
-
-
-def attend(terms, sources, cosine, sine, pkv, bkv, parents, lengths, groups):
+                for c in range(out_ref.shape[0]):
+                    out_ref[c, h // given, 0, :, lanes] = part[r * beams : (r + 1) * beams]
+
+
+def attend(terms, sources, cosine, sine, pkv, bkv, parents, lengths, groups, copies):
     prompts, context, width = pkv.shape
     past = bkv.shape[0] // prompts
     count, _, beams, columns = terms.shape
@@ -135,7 +134,7 @@
             pl.BlockSpec((past, width), lambda i, *_: (i, 0)),
         ],
         out_specs=[
-            pl.BlockSpec((groups, 1, beams, given), lambda i, *_: (0, i, 0, 0)),
+            pl.BlockSpec((copies, groups, 1, beams, given), lambda i, *_: (0, 0, i, 0, 0)),
             pl.BlockSpec((1, beams, width), lambda i, *_: (i, 0, 0)),
         ],
         scratch_shapes=[pltpu.VMEM((slabs, beams, columns), jnp.float32)],
@@ -144,7 +143,7 @@
         attend_kernel,
         grid_spec=grid_spec,
         out_shape=[
-            jax.ShapeDtypeStruct((groups, prompts, beams, given), jnp.bfloat16),
+            jax.ShapeDtypeStruct((copies, groups, prompts, beams, given), jnp.bfloat16),
             jax.ShapeDtypeStruct((prompts, beams, width), jnp.bfloat16),
         ],
         compiler_params=pltpu.CompilerParams(vmem_limit_bytes=56 * 1024 * 1024),
@@ -156,57 +155,102 @@
     )(parents, lengths, sources, terms, cosine, sine, pkv, bkv)
 
 
-def project_kernel(which_ref, places_ref, *refs):
-    *row_refs, own_ref, other_ref, out_ref, row_buffer, weight_buffer, row_sems, weight_sem = refs
+def project_kernel(core_ref, places_ref, *refs):
+    *row_refs, own_ref, other_ref, mine_ref, away_ref = refs[:-7]
+    row_buffer, weight_buffer, mine_buffer, away_buffer, row_sems, weight_sems, out_sems = refs[-7:]
     count, rows, depth = row_buffer.shape
-    for which, ref in enumerate((own_ref, other_ref)):
-
-        @pl.when(which_ref[0] == which)
-        def _(ref=ref):
-            pltpu.make_async_copy(ref, weight_buffer, weight_sem).start()
-
-    copies, at = [], 0
+    half = count // 2
+
+    def fetch(i):
+        for core, pair in enumerate(((own_ref, other_ref), (other_ref, own_ref))):
+
+            @pl.when(core_ref[0] == core)
+            def _(pair=pair):
+                pltpu.make_async_copy(pair[i], weight_buffer.at[i], weight_sems.at[i]).start()
+
+    arriving, at = [[], []], 0
     for s, ref in enumerate(row_refs):
+        if s == 0:
+            fetch(1)
+        elif s == len(row_refs) // 2:
+            fetch(0)
         piece = row_buffer.at[at // rows, pl.ds(at % rows, ref.shape[0])]
-        copies.append(pltpu.make_async_copy(ref, piece, row_sems.at[s]))
-        copies[-1].start()
+        copy = pltpu.make_async_copy(ref, piece, row_sems.at[s])
+        copy.start()
+        arriving[at // (half * rows)].append(copy)
         at += ref.shape[0]
-    pltpu.make_async_copy(own_ref, weight_buffer, weight_sem).wait()
-    for copy in copies:
+    leaving = []
+    for i, buffer, out_ref in ((1, away_buffer, away_ref), (0, mine_buffer, mine_ref)):
+        pltpu.make_async_copy(own_ref, weight_buffer.at[i], weight_sems.at[i]).wait()
+        for h in range(2):
+            if i == 1:
+                for copy in arriving[h]:
+                    copy.wait()
+            product = jnp.dot(
+                row_buffer[h * half : (h + 1) * half].reshape(half * rows, depth),
+                weight_buffer[i],
+                preferred_element_type=jnp.float32,
+            ).astype(jnp.bfloat16)
+            for s in range(half):
+                k = h * half + s
+                buffer[k] = product[s * rows : (s + 1) * rows]
+                copy = pltpu.make_async_copy(
+                    buffer.at[k], out_ref.at[places_ref[k]], out_sems.at[i * count + k]
+                )
+                copy.start()
+                leaving.append(copy)
+    for copy in leaving:
         copy.wait()
-    product = jnp.dot(
-        row_buffer[...].reshape(count * rows, depth),
-        weight_buffer[...],
-        preferred_element_type=jnp.float32,
-    ).astype(jnp.bfloat16)
-    for s in range(count):
-        out_ref[places_ref[s]] = product[s * rows : (s + 1) * rows]
-
-
-def project(which, places, gathered, own, other):
+
+
+def project(core, places, gathered, own, other):
     rows, depth = gathered[0].shape
     count = sum(part.shape[0] for part in gathered) // rows
     columns = own.shape[1]
     scalars = pl.BlockSpec(memory_space=pltpu.SMEM)
+    far = pl.BlockSpec(memory_space=pl.ANY)
     return pl.pallas_call(
         project_kernel,
-        in_specs=[scalars, scalars]
-        + [pl.BlockSpec(memory_space=pl.ANY)] * (len(gathered) + 2),
-        out_specs=pl.BlockSpec(memory_space=pltpu.VMEM),
-        out_shape=jax.ShapeDtypeStruct((count, rows, columns), jnp.bfloat16),
+        in_specs=[scalars, scalars] + [far] * (len(gathered) + 2),
+        out_specs=[far, far],
+        out_shape=[jax.ShapeDtypeStruct((count, rows, columns), jnp.bfloat16)] * 2,
         scratch_shapes=[
             pltpu.VMEM((count, rows, depth), jnp.bfloat16),
-            pltpu.VMEM((depth, columns), jnp.bfloat16),
+            pltpu.VMEM((2, depth, columns), jnp.bfloat16),
+            pltpu.VMEM((count, rows, columns), jnp.bfloat16),
+            pltpu.VMEM((count, rows, columns), jnp.bfloat16),
             pltpu.SemaphoreType.DMA((len(gathered),)),
-            pltpu.SemaphoreType.DMA,
+            pltpu.SemaphoreType.DMA((2,)),
+            pltpu.SemaphoreType.DMA((2 * count,)),
         ],
         compiler_params=pltpu.CompilerParams(vmem_limit_bytes=56 * 1024 * 1024),
         cost_estimate=pl.CostEstimate(
-            flops=2 * count * rows * depth * columns,
-            bytes_accessed=2 * (count * rows * (depth + columns) + depth * columns),
+            flops=4 * count * rows * depth * columns,
+            bytes_accessed=2 * (count * rows * (depth + 2 * columns) + 2 * depth * columns),
             transcendentals=0,
         ),
-    )(which.reshape(1), places, *gathered, own, other)
+    )(core.reshape(1), places, *gathered, own, other)
+
+
+def add_kernel(a_ref, b_ref, out_ref):
+    total = a_ref[...].astype(jnp.float32) + b_ref[...].astype(jnp.float32)
+    out_ref[...] = total.astype(jnp.bfloat16)
+
+
+def add(a, b):
+    count, rows, columns = a.shape
+    block = pl.BlockSpec((2, rows, columns), lambda i: (i, 0, 0))
+    return pl.pallas_call(
+        add_kernel,
+        grid=(count // 2,),
+        in_specs=[block, block],
+        out_specs=block,
+        out_shape=jax.ShapeDtypeStruct(a.shape, jnp.bfloat16),
+        compiler_params=pltpu.CompilerParams(vmem_limit_bytes=24 * 1024 * 1024),
+        cost_estimate=pl.CostEstimate(
+            flops=count * rows * columns, bytes_accessed=6 * count * rows * columns, transcendentals=0
+        ),
+    )(a, b)
 
 
 def output_kernel(core_ref, rows_ref, weight_ref, *refs):
@@ -297,11 +341,8 @@
     places = jnp.concatenate([from_z * 2 + y % 2, from_z * 2 + 1 - y % 2]).astype(jnp.int32)
     core = core.astype(jnp.int32)
 
-    gathered = own + swapped
-    away = project(1 - core, places, gathered, qkv_weight, other)
-    arrived = lax.ppermute(away, "core", SWAP)
-    mine = project(core, places, gathered, qkv_weight, other)
-    terms = (mine.astype(jnp.float32) + arrived.astype(jnp.float32)).astype(jnp.bfloat16)
+    mine, away = project(core, places, own + swapped, qkv_weight, other)
+    terms = add(mine, lax.ppermute(away, "core", SWAP))
     terms = terms.reshape(nx * nz * ny, mine_rows, columns)
     terms = lax.all_to_all(terms, ("x", "z", "y"), split_axis=0, concat_axis=0, tiled=True)
     terms = jnp.sum(terms.reshape(nx, nz, 2, 2, mine_rows, columns).astype(jnp.float32), axis=0)
@@ -311,10 +352,9 @@
     terms = jnp.stack([kept, lax.ppermute(passed, "core", SWAP)])
     terms = terms.reshape(4 * nz, prompts, beams, columns)
     out, fresh = attend(
-        terms, sources, cosine, sine, prompt_key_value, history, parents, lengths, nz
-    )
-    out = out.reshape(nz, mine_rows, -1)
-    copies = jnp.broadcast_to(out[None], (nx,) + out.shape).reshape((nx * nz,) + out.shape[1:])
+        terms, sources, cosine, sine, prompt_key_value, history, parents, lengths, nz, nx
+    )
+    copies = out.reshape(nx * nz, mine_rows, -1)
     mine = lax.all_to_all(copies, ("x", "z"), split_axis=0, concat_axis=0, tiled=True)
     mine = mine.reshape(nx * nz * mine_rows, -1)
     twin = lax.ppermute(mine, "core", SWAP)

time: 196 us -> 194 us (0.990)
  waiting for transfers between devices: 48 us -> 51.6 us
  other arithmetic: 6.63 us -> 3.16 us
    ppermute x1, waiting for transfers between devices: 0.01 us -> 3.79 us  [body(): terms = add(mine, lax.ppermute(away, 'core', SWAP))]
    convert_element_type x1 -> x0, other arithmetic: 3.5 us -> none  [body(): (mine.astype(jnp.float32) + arrived.astype(jnp.float32)).astype(jnp.bfloa...]
    unnamed x26 -> x28, local copies, waits for them, and re-layouts: 2.91 us -> 4.45 us
  transfers between devices with their start and end apart: 15 -> 15, of which waited for: 6 -> 7; matrix products, arithmetic and copies ran while one was open for 4% -> 2% of each run, Pallas kernels for 12% -> 10%
where the time goes in v3:
time: 194 us
  blocking collectives  54.2 us (28%)
  waiting for transfers between devices  51.6 us (27%)
  starting transfers between devices  32.4 us (17%)
  Pallas kernels  31.8 us (16%)
  between operations  14.3 us (7%)
  local copies, waits for them, and re-layouts  6.46 us (3%)
  other arithmetic  3.16 us (2%)
    all_to_all x1, waiting for transfers between devices, body(): lax.all_to_all(terms, ('x', 'z', 'y'), split_axis=0, concat_axis=0, tiled...  29.1 us
    all_to_all x1, blocking collectives, body(): lax.all_to_all(copies, ('x', 'z'), split_axis=0, concat_axis=0, tiled=True)  28.9 us
    all_to_all x1, blocking collectives, body(): lax.all_to_all(product, ('z', 'y'), split_axis=0, concat_axis=0, tiled=True)  25.4 us
    ppermute x8, waiting for transfers between devices, shifted(): lax.ppermute(value, axis, [(i, (i + shift) % size) for i in range(size)])  15.7 us
    pallas_call x1, Pallas kernels, attend(): pl.pallas_call(attend_kernel, grid_spec=grid_spec, out_shape=[jax.ShapeDt...  13.7 us
    ppermute x8, starting transfers between devices, shifted(): lax.ppermute(value, axis, [(i, (i + shift) % size) for i in range(size)])  12 us
    pallas_call x1, Pallas kernels, project(): pl.pallas_call(project_kernel, in_specs=[scalars, scalars] + [far] * (len...  10.1 us
    all_to_all x1, starting transfers between devices, body(): lax.all_to_all(terms, ('x', 'z', 'y'), split_axis=0, concat_axis=0, tiled...  7.91 us
  transfers between devices with their start and end apart: 15, of which 7 were waited for; matrix products, arithmetic and copies ran while one was open for 2% of the time, Pallas kernels for 10%

profile of v3, /device:TPU:1, one launch (start us, length us, event | category | flops | bytes accessed | tf_op | source)
XLA Modules:
  0.0 193.9 jit_solution(12655453556809938183)
XLA Ops:
  7.2 3.6 %collective-permute-start.9 = (bf16[1024,640]{1,0:T(8,128)(2,1)}, bf16[1024,640]{1,0:T(8,128)(2,1)S(1)}, u32[]{:S(2)}, u32[]{:S(2)}) collective-permute-start(bf16[1024,640]{1,0:T(8,128)(2,1)} %refs_10_.1), channel_id=1, source_target_pairs={{0,3},{1,2},{2,1},{3,0},{4,7},{5,6},{6,5},{7,4},{8,11},{9,10},{10,... | collective-permute-start | bytes 3932168 | tf_op jit(solution)/shard_map/ppermute | solution.py:322
  10.9 1.6 collective-permute-start
  12.5 2.1 %collective-permute-start.1 = (bf16[192,1024]{1,0:T(8,128)(2,1)}, bf16[192,1024]{1,0:T(8,128)(2,1)S(1)}, u32[]{:S(2)}, u32[]{:S(2)}) collective-permute-start(bf16[192,1024]{1,0:T(8,128)(2,1)} %refs_0_), channel_id=1, source_target_pairs={{0,12},{4,0},{8,4},{12,8},{1,13},{5,1},{9,5},{13,9},{2,14},{6,2},{... | collective-permute-start | bytes 1179656 | tf_op jit(solution)/shard_map/ppermute | solution.py:300
  14.6 8.7 %collective-permute-done.refs_1_ = bf16[192,1024]{1,0:T(8,128)(2,1)S(1)} collective-permute-done((bf16[192,1024]{1,0:T(8,128)(2,1)}, bf16[192,1024]{1,0:T(8,128)(2,1)S(1)}, u32[]{:S(2)}, u32[]{:S(2)}) %collective-permute-start) | collective-permute-done | bytes 393248 | tf_op jit(solution)/shard_map/ppermute | solution.py:300
  23.3 0.8 collective-permute-done.2.refs_5_
  24.2 2.7 %collective-permute-start.7 = (bf16[192,1024]{1,0:T(8,128)(2,1)S(1)}, bf16[192,1024]{1,0:T(8,128)(2,1)S(1)}, u32[]{:S(2)}, u32[]{:S(2)}) collective-permute-start(bf16[192,1024]{1,0:T(8,128)(2,1)S(1)} %collective-permute-done.2.refs_5_), channel_id=1, source_target_pairs={{0,12},{4,0},{8,4},{12,8},{1,13},{5,1},{9,5},{13,9},{2,14},{6,2},{... | collective-permute-start | bytes 1179656 | tf_op jit(solution)/shard_map/ppermute | solution.py:300
  27.0 2.7 %collective-permute-start.4 = (bf16[96,1024]{1,0:T(8,128)(2,1)S(1)}, bf16[96,1024]{1,0:T(8,128)(2,1)S(1)}, u32[]{:S(2)}, u32[]{:S(2)}) collective-permute-start(bf16[96,1024]{1,0:T(8,128)(2,1)S(1)} %slice.13), channel_id=1, source_target_pairs={{0,12},{4,0},{8,4},{12,8},{1,13},{5,1},{9,5},{13,9},{2,14},{6,2},{... | collective-permute-start | bytes 589832 | tf_op jit(solution)/shard_map/ppermute | solution.py:300
  29.7 4.1 %collective-permute-done.5.refs_6_ = bf16[192,1024]{1,0:T(8,128)(2,1)S(1)} collective-permute-done((bf16[192,1024]{1,0:T(8,128)(2,1)S(1)}, bf16[192,1024]{1,0:T(8,128)(2,1)S(1)}, u32[]{:S(2)}, u32[]{:S(2)}) %collective-permute-start.5) | collective-permute-done | bytes 393248 | tf_op jit(solution)/shard_map/ppermute | solution.py:300
  34.0 2.7 %collective-permute-start.8 = (bf16[96,1024]{1,0:T(8,128)(2,1)S(1)}, bf16[96,1024]{1,0:T(8,128)(2,1)S(1)}, u32[]{:S(2)}, u32[]{:S(2)}) collective-permute-start(bf16[96,1024]{1,0:T(8,128)(2,1)S(1)} %slice.17), channel_id=1, source_target_pairs={{0,12},{4,0},{8,4},{12,8},{1,13},{5,1},{9,5},{13,9},{2,14},{6,2},{... | collective-permute-start | bytes 589832 | tf_op jit(solution)/shard_map/ppermute | solution.py:300
  36.7 0.6 pad_add_fusion.places_ref
  37.3 2.1 %collective-permute-done.9.refs_11_ = bf16[1024,640]{1,0:T(8,128)(2,1)S(1)} collective-permute-done((bf16[1024,640]{1,0:T(8,128)(2,1)}, bf16[1024,640]{1,0:T(8,128)(2,1)S(1)}, u32[]{:S(2)}, u32[]{:S(2)}) %collective-permute-start.9) | collective-permute-done | bytes 1310752 | tf_op jit(solution)/shard_map/ppermute | solution.py:322
  39.4 2.8 %collective-permute-done.6.refs_7_ = bf16[96,1024]{1,0:T(8,128)(2,1)S(1)} collective-permute-done((bf16[96,1024]{1,0:T(8,128)(2,1)S(1)}, bf16[96,1024]{1,0:T(8,128)(2,1)S(1)}, u32[]{:S(2)}, u32[]{:S(2)}) %collective-permute-start.6) | collective-permute-done | bytes 196640 | tf_op jit(solution)/shard_map/ppermute | solution.py:300
  42.4 0.6 copy-done.12
  43.0 10.1 %shard_map.86 = (bf16[8,192,640]{2,1,0:T(8,128)(2,1)}, bf16[8,192,640]{2,1,0:T(8,128)(2,1)}) custom-call(s32[1]{0:T(128)} %bitcast.1.core_ref, s32[8]{0:T(128)} %pad_add_fusion.places_ref, bf16[192,1024]{1,0:T(8,128)(2,1)} %refs_0_, bf16[192,1024]{1,0:T(8,128)(2,1)} %copy-done.3, bf16[96,1024]{1,0:T(8,128)(2,1)} %copy-done.10, bf16[96,1024]{1,0:T(8,128)(2,1)} %copy-done.11, ...), custom_call_target="tpu_custom_call" | custom-call | flops 4026531840 | bytes 9699328 | tf_op jit(solution)/shard_map/pallas_call | solution.py:212
  53.1 4.4 %collective-permute-start.10 = (bf16[8,192,640]{2,1,0:T(8,128)(2,1)}, bf16[8,192,640]{2,1,0:T(8,128)(2,1)S(1)}, u32[]{:S(2)}, u32[]{:S(2)}) collective-permute-start(bf16[8,192,640]{2,1,0:T(8,128)(2,1)} %get-tuple-element.18), channel_id=1, source_target_pairs={{0,16},{16,0},{1,17},{17,1},{2,18},{18,2},{3,19},{19,3},{4,20},{20... | collective-permute-start | bytes 5898248 | tf_op jit(solution)/shard_map/ppermute | solution.py:345
  57.6 3.8 %collective-permute-done.10.b_ref = bf16[8,192,640]{2,1,0:T(8,128)(2,1)S(1)} collective-permute-done((bf16[8,192,640]{2,1,0:T(8,128)(2,1)}, bf16[8,192,640]{2,1,0:T(8,128)(2,1)S(1)}, u32[]{:S(2)}, u32[]{:S(2)}) %collective-permute-start.10) | collective-permute-done | bytes 1966112 | tf_op jit(solution)/shard_map/ppermute | solution.py:345
  61.3 1.5 copy-done.2
  62.9 2.0 %shard_map.87 = bf16[8,192,640]{2,1,0:T(8,128)(2,1)} custom-call(bf16[8,192,640]{2,1,0:T(8,128)(2,1)S(1)} %copy-done.2, bf16[8,192,640]{2,1,0:T(8,128)(2,1)S(1)} %collective-permute-done.10.b_ref), custom_call_target="tpu_custom_call" | custom-call | flops 983040 | bytes 5898240 | tf_op jit(solution)/shard_map/pallas_call | solution.py:243
  64.9 7.9 %all-to-all-start = ((bf16[64,24,640]{2,1,0:T(8,128)(2,1)}), bf16[64,24,640]{2,1,0:T(8,128)(2,1)S(1)}, u32[]{:S(2)}, u32[]{:S(2)}) async-start(bf16[64,24,640]{2,1,0:T(8,128)(2,1)} %bitcast.2), calls=%async_computation | async-start | bytes 3932160 | tf_op jit(solution)/shard_map/all_to_all | solution.py:347
  73.0 29.1 %all-to-all-done = bf16[64,24,640]{2,1,0:T(8,128)(2,1)S(1)} async-done(((bf16[64,24,640]{2,1,0:T(8,128)(2,1)}), bf16[64,24,640]{2,1,0:T(8,128)(2,1)S(1)}, u32[]{:S(2)}, u32[]{:S(2)}) %all-to-all-start) | async-done | bytes 1966112 | tf_op jit(solution)/shard_map/all_to_all | solution.py:347
  102.7 2.1 %collective-permute-start.11 = (bf16[4,2,24,640]{3,2,1,0:T(8,128)(2,1)S(1)}, bf16[4,2,24,640]{3,2,1,0:T(8,128)(2,1)S(1)}, u32[]{:S(2)}, u32[]{:S(2)}) collective-permute-start(bf16[4,2,24,640]{3,2,1,0:T(8,128)(2,1)S(1)} %get-tuple-element.23), channel_id=1, source_target_pairs={{0,16},{16,0},{1,17},{17,1},{2,18},{18,2},{3,19},{19,3},{4,20},{20... | collective-permute-start | bytes 737288 | tf_op jit(solution)/shard_map/ppermute | solution.py:352
  104.9 0.6 copy.12.cos_ref
  106.1 0.6 fusion.sources_ref
  106.7 0.8 pad_maximum_fusion
  107.5 13.7 %shard_map.88 = (bf16[4,4,3,8,2048]{4,3,2,1,0:T(8,128)(2,1)}, bf16[3,8,2048]{2,1,0:T(8,128)(2,1)}) custom-call(s32[24]{0:T(128)} %parents_ref.1, s32[3]{0:T(128)} %lengths_ref.1, s32[16]{0:T(128)} %fusion.sources_ref, bf16[16,3,8,640]{3,2,1,0:T(8,128)(2,1)} %bitcast.26, f32[3,1,128]{2,1,0:T(1,128)} %copy.12.cos_ref, f32[3,1,128]{2,1,0:T(1,128)} %broadcast_in_dim.15.sin_ref, ...), custom_call_target="tpu_custom_call" | custom-call | flops 1308622848 | bytes 20447232 | tf_op jit(solution)/shard_map/pallas_call | solution.py:142
  121.3 28.9 %all_to_all.15 = bf16[16,24,2048]{2,1,0:T(8,128)(2,1)S(1)} all-to-all(bf16[16,24,2048]{2,1,0:T(8,128)(2,1)} %bitcast.27), channel_id=1, replica_groups=mesh['x'=4,'core'=2,'z'=4,'y'=4] {'x','z'}, dimensions={0} | all-to-all | bytes 3145728 | tf_op jit(solution)/shard_map/all_to_all | solution.py:358
  150.1 2.3 %collective-permute-start.12 = (bf16[384,2048]{1,0:T(8,128)(2,1)S(1)}, bf16[384,2048]{1,0:T(8,128)(2,1)S(1)}, u32[]{:S(2)}, u32[]{:S(2)}) collective-permute-start(bf16[384,2048]{1,0:T(8,128)(2,1)S(1)} %bitcast.21), channel_id=1, source_target_pairs={{0,16},{16,0},{1,17},{17,1},{2,18},{18,2},{3,19},{19,3},{4,20},{20... | collective-permute-start | bytes 4718600 | tf_op jit(solution)/shard_map/ppermute | solution.py:360
  152.5 2.2 %copy-done = bf16[2048,1024]{1,0:T(8,128)(2,1)S(1)} copy-done((bf16[2048,1024]{1,0:T(8,128)(2,1)S(1)}, bf16[2048,1024]{1,0:T(8,128)(2,1)}, u32[]{:S(2)}) %copy-start) | copy-done | bytes 4194328
  154.6 3.0 %shard_map.89.refs_0_ = bf16[4,2,96,1024]{3,2,1,0:T(8,128)(2,1)S(1)} custom-call(s32[1]{0:T(128)} %bitcast.1.core_ref, bf16[384,2048]{1,0:T(8,128)(2,1)S(1)} %bitcast.22, bf16[2048,1024]{1,0:T(8,128)(2,1)S(1)} %copy-done), custom_call_target="tpu_custom_call" | custom-call | flops 1610612736 | bytes 6553600 | tf_op jit(solution)/shard_map/pallas_call | solution.py:281
  157.6 3.0 %shard_map.90 = bf16[4,2,96,1024]{3,2,1,0:T(8,128)(2,1)S(1)} custom-call(s32[1]{0:T(128)} %bitcast.core_ref, bf16[384,2048]{1,0:T(8,128)(2,1)S(1)} %collective-permute-done.12.rows_ref, bf16[2048,1024]{1,0:T(8,128)(2,1)S(1)} %copy-done.1, bf16[4,2,96,1024]{3,2,1,0:T(8,128)(2,1)S(1)} %shard_map.89.refs_0_), custom_call_target="tpu_custom_call", output_to_operand_aliasing={{}: (3, {})} | custom-call | flops 1610612736 | bytes 6553600 | tf_op jit(solution)/shard_map/pallas_call | solution.py:281
  160.6 25.4 %all_to_all.16 = bf16[16,48,1024]{2,1,0:T(8,128)(2,1)S(1)} all-to-all(bf16[16,48,1024]{2,1,0:T(8,128)(2,1)S(1)} %bitcast.20), channel_id=1, replica_groups=mesh['x'=4,'core'=2,'z'=4,'y'=4] {'z','y'}, dimensions={0} | all-to-all | bytes 3145728 | tf_op jit(solution)/shard_map/all_to_all | solution.py:364
  186.3 0.8 copy.13
  (53 shorter events, 2.2 us)
Async XLA Ops:
  7.2 145.3 %all-gather.2.cloned.1.call-start = ((), (), s32[]{:S(2)}) async-start(), calls=%async_computation.3 | async-start | bytes 5242880 | tf_op jit(solution)/shard_map/all_gather | solution.py:330
  7.2 32.2 %collective-permute-start.9 = (bf16[1024,640]{1,0:T(8,128)(2,1)}, bf16[1024,640]{1,0:T(8,128)(2,1)S(1)}, u32[]{:S(2)}, u32[]{:S(2)}) collective-permute-start(bf16[1024,640]{1,0:T(8,128)(2,1)} %refs_10_.1), channel_id=1, source_target_pairs={{0,3},{1,2},{2,1},{3,0},{4,7},{5,6},{6,5},{7,4},{8,11},{9,10},{10,... | collective-permute-start | bytes 3932168 | tf_op jit(solution)/shard_map/ppermute | solution.py:322
  10.9 12.5 %collective-permute-start = (bf16[192,1024]{1,0:T(8,128)(2,1)}, bf16[192,1024]{1,0:T(8,128)(2,1)S(1)}, u32[]{:S(2)}, u32[]{:S(2)}) collective-permute-start(bf16[192,1024]{1,0:T(8,128)(2,1)} %refs_0_), channel_id=1, source_target_pairs={{0,4},{4,8},{8,12},{12,0},{1,5},{5,9},{9,13},{13,1},{2,6},{6,10},{... | collective-permute-start | bytes 1179656 | tf_op jit(solution)/shard_map/ppermute | solution.py:300
  12.5 10.9 %collective-permute-start.1 = (bf16[192,1024]{1,0:T(8,128)(2,1)}, bf16[192,1024]{1,0:T(8,128)(2,1)S(1)}, u32[]{:S(2)}, u32[]{:S(2)}) collective-permute-start(bf16[192,1024]{1,0:T(8,128)(2,1)} %refs_0_), channel_id=1, source_target_pairs={{0,12},{4,0},{8,4},{12,8},{1,13},{5,1},{9,5},{13,9},{2,14},{6,2},{... | collective-permute-start | bytes 1179656 | tf_op jit(solution)/shard_map/ppermute | solution.py:300
  14.6 9.6 %collective-permute-start.2 = (bf16[192,1024]{1,0:T(8,128)(2,1)}, bf16[192,1024]{1,0:T(8,128)(2,1)S(1)}, u32[]{:S(2)}, u32[]{:S(2)}) collective-permute-start(bf16[192,1024]{1,0:T(8,128)(2,1)} %refs_0_), channel_id=1, source_target_pairs={{0,1},{1,0},{2,3},{3,2},{4,5},{5,4},{6,7},{7,6},{8,9},{9,8},{10,11... | collective-permute-start | bytes 1179656 | tf_op jit(solution)/shard_map/ppermute | solution.py:324
  23.3 18.9 %copy-start.3 = (bf16[192,1024]{1,0:T(8,128)(2,1)}, bf16[192,1024]{1,0:T(8,128)(2,1)S(1)}, u32[]{:S(2)}) copy-start(bf16[192,1024]{1,0:T(8,128)(2,1)S(1)} %collective-permute-done.refs_1_) | copy-start | bytes 1179652
  23.3 18.9 %copy-start.4 = (bf16[192,1024]{1,0:T(8,128)(2,1)}, bf16[192,1024]{1,0:T(8,128)(2,1)S(1)}, u32[]{:S(2)}) copy-start(bf16[192,1024]{1,0:T(8,128)(2,1)S(1)} %collective-permute-done.1.refs_4_) | copy-start | bytes 1179652
  24.2 18.1 %copy-start.9 = (bf16[192,1024]{1,0:T(8,128)(2,1)}, bf16[192,1024]{1,0:T(8,128)(2,1)S(1)}, u32[]{:S(2)}) copy-start(bf16[192,1024]{1,0:T(8,128)(2,1)S(1)} %collective-permute-done.2.refs_5_) | copy-start | bytes 1179652
  24.2 9.7 %collective-permute-start.5 = (bf16[192,1024]{1,0:T(8,128)(2,1)S(1)}, bf16[192,1024]{1,0:T(8,128)(2,1)S(1)}, u32[]{:S(2)}, u32[]{:S(2)}) collective-permute-start(bf16[192,1024]{1,0:T(8,128)(2,1)S(1)} %collective-permute-done.2.refs_5_), channel_id=1, source_target_pairs={{0,4},{4,8},{8,12},{12,0},{1,5},{5,9},{9,13},{13,1},{2,6},{6,10},{... | collective-permute-start | bytes 1179656 | tf_op jit(solution)/shard_map/ppermute | solution.py:300
  24.2 9.8 %collective-permute-start.7 = (bf16[192,1024]{1,0:T(8,128)(2,1)S(1)}, bf16[192,1024]{1,0:T(8,128)(2,1)S(1)}, u32[]{:S(2)}, u32[]{:S(2)}) collective-permute-start(bf16[192,1024]{1,0:T(8,128)(2,1)S(1)} %collective-permute-done.2.refs_5_), channel_id=1, source_target_pairs={{0,12},{4,0},{8,4},{12,8},{1,13},{5,1},{9,5},{13,9},{2,14},{6,2},{... | collective-permute-start | bytes 1179656 | tf_op jit(solution)/shard_map/ppermute | solution.py:300
  26.9 12.5 %collective-permute-start.3 = (bf16[96,1024]{1,0:T(8,128)(2,1)S(1)}, bf16[96,1024]{1,0:T(8,128)(2,1)S(1)}, u32[]{:S(2)}, u32[]{:S(2)}) collective-permute-start(bf16[96,1024]{1,0:T(8,128)(2,1)S(1)} %slice.12), channel_id=1, source_target_pairs={{0,4},{4,8},{8,12},{12,0},{1,5},{5,9},{9,13},{13,1},{2,6},{6,10},{... | collective-permute-start | bytes 589832 | tf_op jit(solution)/shard_map/ppermute | solution.py:300
  27.0 12.4 %collective-permute-start.4 = (bf16[96,1024]{1,0:T(8,128)(2,1)S(1)}, bf16[96,1024]{1,0:T(8,128)(2,1)S(1)}, u32[]{:S(2)}, u32[]{:S(2)}) collective-permute-start(bf16[96,1024]{1,0:T(8,128)(2,1)S(1)} %slice.13), channel_id=1, source_target_pairs={{0,12},{4,0},{8,4},{12,8},{1,13},{5,1},{9,5},{13,9},{2,14},{6,2},{... | collective-permute-start | bytes 589832 | tf_op jit(solution)/shard_map/ppermute | solution.py:300
  33.9 8.5 %copy-start.5 = (bf16[192,1024]{1,0:T(8,128)(2,1)}, bf16[192,1024]{1,0:T(8,128)(2,1)S(1)}, u32[]{:S(2)}) copy-start(bf16[192,1024]{1,0:T(8,128)(2,1)S(1)} %collective-permute-done.5.refs_6_) | copy-start | bytes 1179652
  33.9 8.4 %collective-permute-start.6 = (bf16[96,1024]{1,0:T(8,128)(2,1)S(1)}, bf16[96,1024]{1,0:T(8,128)(2,1)S(1)}, u32[]{:S(2)}, u32[]{:S(2)}) collective-permute-start(bf16[96,1024]{1,0:T(8,128)(2,1)S(1)} %slice.16), channel_id=1, source_target_pairs={{0,4},{4,8},{8,12},{12,0},{1,5},{5,9},{9,13},{13,1},{2,6},{6,10},{... | collective-permute-start | bytes 589832 | tf_op jit(solution)/shard_map/ppermute | solution.py:300
  34.0 8.4 %copy-start.6 = (bf16[192,1024]{1,0:T(8,128)(2,1)}, bf16[192,1024]{1,0:T(8,128)(2,1)S(1)}, u32[]{:S(2)}) copy-start(bf16[192,1024]{1,0:T(8,128)(2,1)S(1)} %collective-permute-done.7.refs_9_) | copy-start | bytes 1179652
  34.0 8.3 %collective-permute-start.8 = (bf16[96,1024]{1,0:T(8,128)(2,1)S(1)}, bf16[96,1024]{1,0:T(8,128)(2,1)S(1)}, u32[]{:S(2)}, u32[]{:S(2)}) collective-permute-start(bf16[96,1024]{1,0:T(8,128)(2,1)S(1)} %slice.17), channel_id=1, source_target_pairs={{0,12},{4,0},{8,4},{12,8},{1,13},{5,1},{9,5},{13,9},{2,14},{6,2},{... | collective-permute-start | bytes 589832 | tf_op jit(solution)/shard_map/ppermute | solution.py:300
  39.4 2.9 %copy-start.8 = (bf16[1024,640]{1,0:T(8,128)(2,1)}, bf16[1024,640]{1,0:T(8,128)(2,1)S(1)}, u32[]{:S(2)}) copy-start(bf16[1024,640]{1,0:T(8,128)(2,1)S(1)} %collective-permute-done.9.refs_11_) | copy-start | bytes 3932164
  39.4 2.9 %copy-start.10 = (bf16[96,1024]{1,0:T(8,128)(2,1)}, bf16[96,1024]{1,0:T(8,128)(2,1)S(1)}, u32[]{:S(2)}) copy-start(bf16[96,1024]{1,0:T(8,128)(2,1)S(1)} %collective-permute-done.3.refs_2_) | copy-start | bytes 589828
  39.4 2.9 %copy-start.11 = (bf16[96,1024]{1,0:T(8,128)(2,1)}, bf16[96,1024]{1,0:T(8,128)(2,1)S(1)}, u32[]{:S(2)}) copy-start(bf16[96,1024]{1,0:T(8,128)(2,1)S(1)} %collective-permute-done.4.refs_3_) | copy-start | bytes 589828
  42.3 0.7 copy-start.12
  42.3 0.8 copy-start.13
  53.1 8.2 %collective-permute-start.10 = (bf16[8,192,640]{2,1,0:T(8,128)(2,1)}, bf16[8,192,640]{2,1,0:T(8,128)(2,1)S(1)}, u32[]{:S(2)}, u32[]{:S(2)}) collective-permute-start(bf16[8,192,640]{2,1,0:T(8,128)(2,1)} %get-tuple-element.18), channel_id=1, source_target_pairs={{0,16},{16,0},{1,17},{17,1},{2,18},{18,2},{3,19},{19,3},{4,20},{20... | collective-permute-start | bytes 5898248 | tf_op jit(solution)/shard_map/ppermute | solution.py:345
  61.3 1.5 copy-start.2
  64.9 7.9 %copy-start.7 = (s32[3]{0:T(128)S(1)}, s32[3]{0:T(128)}, u32[]{:S(2)}) copy-start(s32[3]{0:T(128)} %lengths_ref.1) | copy-start | bytes 40
  64.9 37.2 %all-to-all-start = ((bf16[64,24,640]{2,1,0:T(8,128)(2,1)}), bf16[64,24,640]{2,1,0:T(8,128)(2,1)S(1)}, u32[]{:S(2)}, u32[]{:S(2)}) async-start(bf16[64,24,640]{2,1,0:T(8,128)(2,1)} %bitcast.2), calls=%async_computation | async-start | bytes 3932160 | tf_op jit(solution)/shard_map/all_to_all | solution.py:347
  102.7 4.0 %collective-permute-start.11 = (bf16[4,2,24,640]{3,2,1,0:T(8,128)(2,1)S(1)}, bf16[4,2,24,640]{3,2,1,0:T(8,128)(2,1)S(1)}, u32[]{:S(2)}, u32[]{:S(2)}) collective-permute-start(bf16[4,2,24,640]{3,2,1,0:T(8,128)(2,1)S(1)} %get-tuple-element.23), channel_id=1, source_target_pairs={{0,16},{16,0},{1,17},{17,1},{2,18},{18,2},{3,19},{19,3},{4,20},{20... | collective-permute-start | bytes 737288 | tf_op jit(solution)/shard_map/ppermute | solution.py:352
  150.1 7.5 %collective-permute-start.12 = (bf16[384,2048]{1,0:T(8,128)(2,1)S(1)}, bf16[384,2048]{1,0:T(8,128)(2,1)S(1)}, u32[]{:S(2)}, u32[]{:S(2)}) collective-permute-start(bf16[384,2048]{1,0:T(8,128)(2,1)S(1)} %bitcast.21), channel_id=1, source_target_pairs={{0,16},{16,0},{1,17},{17,1},{2,18},{18,2},{3,19},{19,3},{4,20},{20... | collective-permute-start | bytes 4718600 | tf_op jit(solution)/shard_map/ppermute | solution.py:360
  152.5 2.2 %copy-start = (bf16[2048,1024]{1,0:T(8,128)(2,1)S(1)}, bf16[2048,1024]{1,0:T(8,128)(2,1)}, u32[]{:S(2)}) copy-start(bf16[2048,1024]{1,0:T(8,128)(2,1)} %all-gather.2.cloned.1.call-done.weight_ref) | copy-start | bytes 12582916
  154.6 3.0 %copy-start.1 = (bf16[2048,1024]{1,0:T(8,128)(2,1)S(1)}, bf16[2048,1024]{1,0:T(8,128)(2,1)}, u32[]{:S(2)}) copy-start(bf16[2048,1024]{1,0:T(8,128)(2,1)} %all-gather.2.cloned.1.call-done.weight_ref) | copy-start | bytes 12582916
Sparse Core Ops, SparseCore 0:
  57.7 67.8 all-gather.1

commit v4 on v3

--- a/solution.py
+++ b/solution.py
@@ -21,10 +21,11 @@
     frequency = jnp.exp(-jnp.log(jnp.float32(500000.0)) * exponent)
     angles = positions.astype(jnp.float32)[:, None] * frequency[None, :]
     cosine, sine = jnp.cos(angles), jnp.sin(angles)
-    return (
-        jnp.concatenate([cosine, cosine], axis=1)[:, None, :],
-        jnp.concatenate([-sine, sine], axis=1)[:, None, :],
-    )
+    rows = [
+        jnp.concatenate([cosine, cosine], axis=1),
+        jnp.concatenate([-sine, sine], axis=1),
+    ]
+    return jnp.concatenate(rows, axis=0)[:, None, :]
 
 
 def attend_kernel(
@@ -117,7 +118,7 @@
                     out_ref[c, h // given, 0, :, lanes] = part[r * beams : (r + 1) * beams]
 
 
-def attend(terms, sources, cosine, sine, pkv, bkv, parents, lengths, groups, copies):
+def attend(terms, sources, tables, pkv, bkv, parents, lengths, groups, copies):
     prompts, context, width = pkv.shape
     past = bkv.shape[0] // prompts
     count, _, beams, columns = terms.shape
@@ -129,7 +130,7 @@
         in_specs=[
             pl.BlockSpec((count, 1, beams, columns), lambda i, *_: (0, i, 0, 0)),
             pl.BlockSpec((1, 1, HEAD_SIZE), lambda i, *_: (i, 0, 0)),
-            pl.BlockSpec((1, 1, HEAD_SIZE), lambda i, *_: (i, 0, 0)),
+            pl.BlockSpec((1, 1, HEAD_SIZE), lambda i, *_: (prompts + i, 0, 0)),
             pl.BlockSpec((1, context, width), lambda i, *_: (i, 0, 0)),
             pl.BlockSpec((past, width), lambda i, *_: (i, 0)),
         ],
@@ -152,7 +153,7 @@
             bytes_accessed=2 * prompts * width * (context + past),
             transcendentals=prompts * 64 * KEY_HEADS * (context + past),
         ),
-    )(parents, lengths, sources, terms, cosine, sine, pkv, bkv)
+    )(parents, lengths, sources, terms, tables, tables, pkv, bkv)
 
 
 def project_kernel(core_ref, places_ref, *refs):
@@ -322,15 +323,7 @@
     other = lax.ppermute(qkv_weight, "y", [(i, ny - 1 - i) for i in range(ny)])
     own = beside(normed, "z")
     swapped = lax.ppermute(normed, "y", [(i, i ^ 1) for i in range(ny)])
-    *own, swapped = lax.optimization_barrier((*own, swapped))
-    swapped = beside(swapped, "z")
-    own = relayed(own, "z")
-    swapped = relayed(swapped, "z")
-    out_weight, other = lax.optimization_barrier((out_weight, other))
-    weight = lax.all_gather(out_weight, "y", axis=0, tiled=True)
-
-    cosine, sine = rotary_tables(lengths + beam_key_value.shape[1])
-    history = beam_key_value.reshape(-1, beam_key_value.shape[-1])
+    tables = rotary_tables(lengths + beam_key_value.shape[1])
     slab = jnp.arange(nz * ny, dtype=jnp.int32)
     slab_z, slab_y = slab // ny, slab % ny
     slots = jnp.where(slab_y // 2 == core, 0, 1)
@@ -340,7 +333,16 @@
     from_z = (z - jnp.arange(nz, dtype=jnp.int32)) % nz
     places = jnp.concatenate([from_z * 2 + y % 2, from_z * 2 + 1 - y % 2]).astype(jnp.int32)
     core = core.astype(jnp.int32)
-
+    small = (tables, sources, places)
+    (*own, swapped), small = lax.optimization_barrier(((*own, swapped), small))
+    tables, sources, places = small
+    swapped = beside(swapped, "z")
+    own = relayed(own, "z")
+    swapped = relayed(swapped, "z")
+    out_weight, other = lax.optimization_barrier((out_weight, other))
+    weight = lax.all_gather(out_weight, "y", axis=0, tiled=True)
+
+    history = beam_key_value.reshape(-1, beam_key_value.shape[-1])
     mine, away = project(core, places, own + swapped, qkv_weight, other)
     terms = add(mine, lax.ppermute(away, "core", SWAP))
     terms = terms.reshape(nx * nz * ny, mine_rows, columns)
@@ -352,7 +354,7 @@
     terms = jnp.stack([kept, lax.ppermute(passed, "core", SWAP)])
     terms = terms.reshape(4 * nz, prompts, beams, columns)
     out, fresh = attend(
-        terms, sources, cosine, sine, prompt_key_value, history, parents, lengths, nz, nx
+        terms, sources, tables, prompt_key_value, history, parents, lengths, nz, nx
     )
     copies = out.reshape(nx * nz, mine_rows, -1)
     mine = lax.all_to_all(copies, ("x", "z"), split_axis=0, concat_axis=0, tiled=True)

time: 194 us -> 193 us (level)
    ppermute x8, waiting for transfers between devices: 15.7 us -> 7.63 us  [shifted(): lax.ppermute(value, axis, [(i, (i + shift) % size) for i in range(size)])]
    ppermute x1, waiting for transfers between devices: 2.11 us -> 9.06 us  [body(): other = lax.ppermute(qkv_weight, 'y', [(i, ny - 1 - i) for i in range(ny)])]
    ppermute x1, starting transfers between devices: 4.38 us -> 2.24 us  [body(): terms = add(mine, lax.ppermute(away, 'core', SWAP))]
    unnamed x28 -> x26, local copies, waits for them, and re-layouts: 4.45 us -> 4.98 us
where the time goes in v4:
time: 193 us
  blocking collectives  54.6 us (28%)
  waiting for transfers between devices  51.8 us (27%)
  Pallas kernels  31.7 us (16%)
  starting transfers between devices  30.5 us (16%)
  between operations  14.3 us (7%)
  local copies, waits for them, and re-layouts  6.48 us (3%)
  other arithmetic  3.65 us (2%)
    all_to_all x1, waiting for transfers between devices, body(): lax.all_to_all(terms, ('x', 'z', 'y'), split_axis=0, concat_axis=0, tiled...  29.3 us
    all_to_all x1, blocking collectives, body(): lax.all_to_all(copies, ('x', 'z'), split_axis=0, concat_axis=0, tiled=True)  29.2 us
    all_to_all x1, blocking collectives, body(): lax.all_to_all(product, ('z', 'y'), split_axis=0, concat_axis=0, tiled=True)  25.4 us
    pallas_call x1, Pallas kernels, attend(): pl.pallas_call(attend_kernel, grid_spec=grid_spec, out_shape=[jax.ShapeDt...  13.7 us
    ppermute x8, starting transfers between devices, shifted(): lax.ppermute(value, axis, [(i, (i + shift) % size) for i in range(size)])  13 us
    pallas_call x1, Pallas kernels, project(): pl.pallas_call(project_kernel, in_specs=[scalars, scalars] + [far] * (len...  10.1 us
    ppermute x1, waiting for transfers between devices, body(): other = lax.ppermute(qkv_weight, 'y', [(i, ny - 1 - i) for i in range(ny)])  9.06 us
    all_to_all x1, starting transfers between devices, body(): lax.all_to_all(terms, ('x', 'z', 'y'), split_axis=0, concat_axis=0, tiled...  7.85 us
  transfers between devices with their start and end apart: 15, of which 7 were waited for; matrix products, arithmetic and copies ran while one was open for 2% of the time, Pallas kernels for 10%

profile of v4, /device:TPU:1, one launch (start us, length us, event | category | flops | bytes accessed | tf_op | source)
XLA Modules:
  0.0 193.0 jit_solution(17239604306247209384)
XLA Ops:
  7.2 2.5 %collective-permute-start = (bf16[192,1024]{1,0:T(8,128)(2,1)}, bf16[192,1024]{1,0:T(8,128)(2,1)S(1)}, u32[]{:S(2)}, u32[]{:S(2)}) collective-permute-start(bf16[192,1024]{1,0:T(8,128)(2,1)} %refs_0_), channel_id=1, source_target_pairs={{0,4},{4,8},{8,12},{12,0},{1,5},{5,9},{9,13},{13,1},{2,6},{6,10},{... | collective-permute-start | bytes 1179656 | tf_op jit(solution)/shard_map/ppermute | solution.py:301
  9.7 2.2 %collective-permute-start.1 = (bf16[192,1024]{1,0:T(8,128)(2,1)}, bf16[192,1024]{1,0:T(8,128)(2,1)S(1)}, u32[]{:S(2)}, u32[]{:S(2)}) collective-permute-start(bf16[192,1024]{1,0:T(8,128)(2,1)} %refs_0_), channel_id=1, source_target_pairs={{0,12},{4,0},{8,4},{12,8},{1,13},{5,1},{9,5},{13,9},{2,14},{6,2},{... | collective-permute-start | bytes 1179656 | tf_op jit(solution)/shard_map/ppermute | solution.py:301
  11.9 1.3 collective-permute-start.2
  13.2 1.9 collective-permute-start.9
  15.1 0.7 add_convert_fusion
  16.0 0.6 broadcast_in_dim.11.cos_ref.sin_ref
  17.7 3.2 %collective-permute-done.refs_1_ = bf16[192,1024]{1,0:T(8,128)(2,1)S(1)} collective-permute-done((bf16[192,1024]{1,0:T(8,128)(2,1)}, bf16[192,1024]{1,0:T(8,128)(2,1)S(1)}, u32[]{:S(2)}, u32[]{:S(2)}) %collective-permute-start) | collective-permute-done | bytes 393248 | tf_op jit(solution)/shard_map/ppermute | solution.py:301
  20.9 0.9 collective-permute-done.2.refs_5_
  21.8 2.7 %collective-permute-start.7 = (bf16[192,1024]{1,0:T(8,128)(2,1)S(1)}, bf16[192,1024]{1,0:T(8,128)(2,1)S(1)}, u32[]{:S(2)}, u32[]{:S(2)}) collective-permute-start(bf16[192,1024]{1,0:T(8,128)(2,1)S(1)} %collective-permute-done.2.refs_5_), channel_id=1, source_target_pairs={{0,12},{4,0},{8,4},{12,8},{1,13},{5,1},{9,5},{13,9},{2,14},{6,2},{... | collective-permute-start | bytes 1179656 | tf_op jit(solution)/shard_map/ppermute | solution.py:301
  24.6 2.7 %collective-permute-start.4 = (bf16[96,1024]{1,0:T(8,128)(2,1)S(1)}, bf16[96,1024]{1,0:T(8,128)(2,1)S(1)}, u32[]{:S(2)}, u32[]{:S(2)}) collective-permute-start(bf16[96,1024]{1,0:T(8,128)(2,1)S(1)} %slice.13), channel_id=1, source_target_pairs={{0,12},{4,0},{8,4},{12,8},{1,13},{5,1},{9,5},{13,9},{2,14},{6,2},{... | collective-permute-start | bytes 589832 | tf_op jit(solution)/shard_map/ppermute | solution.py:301
  27.4 4.4 %collective-permute-done.5.refs_6_ = bf16[192,1024]{1,0:T(8,128)(2,1)S(1)} collective-permute-done((bf16[192,1024]{1,0:T(8,128)(2,1)S(1)}, bf16[192,1024]{1,0:T(8,128)(2,1)S(1)}, u32[]{:S(2)}, u32[]{:S(2)}) %collective-permute-start.5) | collective-permute-done | bytes 393248 | tf_op jit(solution)/shard_map/ppermute | solution.py:301
  31.9 2.7 %collective-permute-start.8 = (bf16[96,1024]{1,0:T(8,128)(2,1)S(1)}, bf16[96,1024]{1,0:T(8,128)(2,1)S(1)}, u32[]{:S(2)}, u32[]{:S(2)}) collective-permute-start(bf16[96,1024]{1,0:T(8,128)(2,1)S(1)} %slice.17), channel_id=1, source_target_pairs={{0,12},{4,0},{8,4},{12,8},{1,13},{5,1},{9,5},{13,9},{2,14},{6,2},{... | collective-permute-start | bytes 589832 | tf_op jit(solution)/shard_map/ppermute | solution.py:301
  34.6 9.1 %collective-permute-done.9.refs_11_ = bf16[1024,640]{1,0:T(8,128)(2,1)S(1)} collective-permute-done((bf16[1024,640]{1,0:T(8,128)(2,1)}, bf16[1024,640]{1,0:T(8,128)(2,1)S(1)}, u32[]{:S(2)}, u32[]{:S(2)}) %collective-permute-start.9) | collective-permute-done | bytes 1310752 | tf_op jit(solution)/shard_map/ppermute | solution.py:323
  43.8 1.0 copy-done.7
  45.0 10.1 %shard_map.86 = (bf16[8,192,640]{2,1,0:T(8,128)(2,1)}, bf16[8,192,640]{2,1,0:T(8,128)(2,1)}) custom-call(s32[1]{0:T(128)} %bitcast.1.core_ref, s32[8]{0:T(128)} %pad_add_fusion.places_ref, bf16[192,1024]{1,0:T(8,128)(2,1)} %refs_0_, bf16[192,1024]{1,0:T(8,128)(2,1)} %copy-done.3, bf16[96,1024]{1,0:T(8,128)(2,1)} %copy-done.9, bf16[96,1024]{1,0:T(8,128)(2,1)} %copy-done.10, ...), custom_call_target="tpu_custom_call" | custom-call | flops 4026531840 | bytes 9699328 | tf_op jit(solution)/shard_map/pallas_call | solution.py:213
  55.1 2.2 %collective-permute-start.10 = (bf16[8,192,640]{2,1,0:T(8,128)(2,1)}, bf16[8,192,640]{2,1,0:T(8,128)(2,1)S(1)}, u32[]{:S(2)}, u32[]{:S(2)}) collective-permute-start(bf16[8,192,640]{2,1,0:T(8,128)(2,1)} %get-tuple-element.23), channel_id=1, source_target_pairs={{0,16},{16,0},{1,17},{17,1},{2,18},{18,2},{3,19},{19,3},{4,20},{20... | collective-permute-start | bytes 5898248 | tf_op jit(solution)/shard_map/ppermute | solution.py:347
  57.4 3.8 %collective-permute-done.10.b_ref = bf16[8,192,640]{2,1,0:T(8,128)(2,1)S(1)} collective-permute-done((bf16[8,192,640]{2,1,0:T(8,128)(2,1)}, bf16[8,192,640]{2,1,0:T(8,128)(2,1)S(1)}, u32[]{:S(2)}, u32[]{:S(2)}) %collective-permute-start.10) | collective-permute-done | bytes 1966112 | tf_op jit(solution)/shard_map/ppermute | solution.py:347
  61.2 1.5 copy-done.2
  62.7 2.0 %shard_map.87 = bf16[8,192,640]{2,1,0:T(8,128)(2,1)} custom-call(bf16[8,192,640]{2,1,0:T(8,128)(2,1)S(1)} %copy-done.2, bf16[8,192,640]{2,1,0:T(8,128)(2,1)S(1)} %collective-permute-done.10.b_ref), custom_call_target="tpu_custom_call" | custom-call | flops 983040 | bytes 5898240 | tf_op jit(solution)/shard_map/pallas_call | solution.py:244
  64.7 7.8 %all-to-all-start = ((bf16[64,24,640]{2,1,0:T(8,128)(2,1)}), bf16[64,24,640]{2,1,0:T(8,128)(2,1)S(1)}, u32[]{:S(2)}, u32[]{:S(2)}) async-start(bf16[64,24,640]{2,1,0:T(8,128)(2,1)} %bitcast.2), calls=%async_computation | async-start | bytes 3932160 | tf_op jit(solution)/shard_map/all_to_all | solution.py:349
  72.6 29.3 %all-to-all-done = bf16[64,24,640]{2,1,0:T(8,128)(2,1)S(1)} async-done(((bf16[64,24,640]{2,1,0:T(8,128)(2,1)}), bf16[64,24,640]{2,1,0:T(8,128)(2,1)S(1)}, u32[]{:S(2)}, u32[]{:S(2)}) %all-to-all-start) | async-done | bytes 1966112 | tf_op jit(solution)/shard_map/all_to_all | solution.py:349
  102.5 2.1 %collective-permute-start.11 = (bf16[4,2,24,640]{3,2,1,0:T(8,128)(2,1)S(1)}, bf16[4,2,24,640]{3,2,1,0:T(8,128)(2,1)S(1)}, u32[]{:S(2)}, u32[]{:S(2)}) collective-permute-start(bf16[4,2,24,640]{3,2,1,0:T(8,128)(2,1)S(1)} %get-tuple-element.29), channel_id=1, source_target_pairs={{0,16},{16,0},{1,17},{17,1},{2,18},{18,2},{3,19},{19,3},{4,20},{20... | collective-permute-start | bytes 737288 | tf_op jit(solution)/shard_map/ppermute | solution.py:354
  104.6 1.1 collective-permute-done.11
  105.7 0.8 pad_maximum_fusion
  106.5 13.7 %shard_map.88 = (bf16[4,4,3,8,2048]{4,3,2,1,0:T(8,128)(2,1)}, bf16[3,8,2048]{2,1,0:T(8,128)(2,1)}) custom-call(s32[24]{0:T(128)} %parents_ref.1, s32[3]{0:T(128)} %lengths_ref.1, s32[16]{0:T(128)} %fusion.sources_ref, bf16[16,3,8,640]{3,2,1,0:T(8,128)(2,1)} %bitcast.24, f32[6,1,128]{2,1,0:T(1,128)} %broadcast_in_dim.11.cos_ref.sin_ref, ...), custom_call_target="tpu_custom_call" | custom-call | flops 1308622848 | bytes 20447232 | tf_op jit(solution)/shard_map/pallas_call | solution.py:143
  120.2 29.2 %all_to_all.15 = bf16[16,24,2048]{2,1,0:T(8,128)(2,1)S(1)} all-to-all(bf16[16,24,2048]{2,1,0:T(8,128)(2,1)} %bitcast.25), channel_id=1, replica_groups=mesh['x'=4,'core'=2,'z'=4,'y'=4] {'x','z'}, dimensions={0} | all-to-all | bytes 3145728 | tf_op jit(solution)/shard_map/all_to_all | solution.py:360
  149.4 2.1 %collective-permute-start.12 = (bf16[384,2048]{1,0:T(8,128)(2,1)S(1)}, bf16[384,2048]{1,0:T(8,128)(2,1)S(1)}, u32[]{:S(2)}, u32[]{:S(2)}) collective-permute-start(bf16[384,2048]{1,0:T(8,128)(2,1)S(1)} %bitcast.19), channel_id=1, source_target_pairs={{0,16},{16,0},{1,17},{17,1},{2,18},{18,2},{3,19},{19,3},{4,20},{20... | collective-permute-start | bytes 4718600 | tf_op jit(solution)/shard_map/ppermute | solution.py:362
  151.5 2.2 %copy-done = bf16[2048,1024]{1,0:T(8,128)(2,1)S(1)} copy-done((bf16[2048,1024]{1,0:T(8,128)(2,1)S(1)}, bf16[2048,1024]{1,0:T(8,128)(2,1)}, u32[]{:S(2)}) %copy-start) | copy-done | bytes 4194328
  153.7 3.0 %shard_map.89.refs_0_ = bf16[4,2,96,1024]{3,2,1,0:T(8,128)(2,1)S(1)} custom-call(s32[1]{0:T(128)} %bitcast.1.core_ref, bf16[384,2048]{1,0:T(8,128)(2,1)S(1)} %bitcast.20, bf16[2048,1024]{1,0:T(8,128)(2,1)S(1)} %copy-done), custom_call_target="tpu_custom_call" | custom-call | flops 1610612736 | bytes 6553600 | tf_op jit(solution)/shard_map/pallas_call | solution.py:282
  156.7 3.0 %shard_map.90 = bf16[4,2,96,1024]{3,2,1,0:T(8,128)(2,1)S(1)} custom-call(s32[1]{0:T(128)} %bitcast.core_ref, bf16[384,2048]{1,0:T(8,128)(2,1)S(1)} %collective-permute-done.12.rows_ref, bf16[2048,1024]{1,0:T(8,128)(2,1)S(1)} %copy-done.1, bf16[4,2,96,1024]{3,2,1,0:T(8,128)(2,1)S(1)} %shard_map.89.refs_0_), custom_call_target="tpu_custom_call", output_to_operand_aliasing={{}: (3, {})} | custom-call | flops 1610612736 | bytes 6553600 | tf_op jit(solution)/shard_map/pallas_call | solution.py:282
  159.7 25.4 %all_to_all.16 = bf16[16,48,1024]{2,1,0:T(8,128)(2,1)S(1)} all-to-all(bf16[16,48,1024]{2,1,0:T(8,128)(2,1)S(1)} %bitcast.18), channel_id=1, replica_groups=mesh['x'=4,'core'=2,'z'=4,'y'=4] {'z','y'}, dimensions={0} | all-to-all | bytes 3145728 | tf_op jit(solution)/shard_map/all_to_all | solution.py:366
  185.4 0.8 copy.10
  (49 shorter events, 2.8 us)
Async XLA Ops:
  7.2 144.4 %all-gather.2.cloned.1.call-start = ((), (), s32[]{:S(2)}) async-start(), calls=%async_computation.3 | async-start | bytes 5242880 | tf_op jit(solution)/shard_map/all_gather | solution.py:343
  7.2 13.7 %collective-permute-start = (bf16[192,1024]{1,0:T(8,128)(2,1)}, bf16[192,1024]{1,0:T(8,128)(2,1)S(1)}, u32[]{:S(2)}, u32[]{:S(2)}) collective-permute-start(bf16[192,1024]{1,0:T(8,128)(2,1)} %refs_0_), channel_id=1, source_target_pairs={{0,4},{4,8},{8,12},{12,0},{1,5},{5,9},{9,13},{13,1},{2,6},{6,10},{... | collective-permute-start | bytes 1179656 | tf_op jit(solution)/shard_map/ppermute | solution.py:301
  9.7 11.2 %collective-permute-start.1 = (bf16[192,1024]{1,0:T(8,128)(2,1)}, bf16[192,1024]{1,0:T(8,128)(2,1)S(1)}, u32[]{:S(2)}, u32[]{:S(2)}) collective-permute-start(bf16[192,1024]{1,0:T(8,128)(2,1)} %refs_0_), channel_id=1, source_target_pairs={{0,12},{4,0},{8,4},{12,8},{1,13},{5,1},{9,5},{13,9},{2,14},{6,2},{... | collective-permute-start | bytes 1179656 | tf_op jit(solution)/shard_map/ppermute | solution.py:301
  11.9 9.9 %collective-permute-start.2 = (bf16[192,1024]{1,0:T(8,128)(2,1)}, bf16[192,1024]{1,0:T(8,128)(2,1)S(1)}, u32[]{:S(2)}, u32[]{:S(2)}) collective-permute-start(bf16[192,1024]{1,0:T(8,128)(2,1)} %refs_0_), channel_id=1, source_target_pairs={{0,1},{1,0},{2,3},{3,2},{4,5},{5,4},{6,7},{7,6},{8,9},{9,8},{10,11... | collective-permute-start | bytes 1179656 | tf_op jit(solution)/shard_map/ppermute | solution.py:325
  13.2 30.5 %collective-permute-start.9 = (bf16[1024,640]{1,0:T(8,128)(2,1)}, bf16[1024,640]{1,0:T(8,128)(2,1)S(1)}, u32[]{:S(2)}, u32[]{:S(2)}) collective-permute-start(bf16[1024,640]{1,0:T(8,128)(2,1)} %refs_10_.1), channel_id=1, source_target_pairs={{0,3},{1,2},{2,1},{3,0},{4,7},{5,6},{6,5},{7,4},{8,11},{9,10},{10,... | collective-permute-start | bytes 3932168 | tf_op jit(solution)/shard_map/ppermute | solution.py:323
  20.9 22.8 %copy-start.3 = (bf16[192,1024]{1,0:T(8,128)(2,1)}, bf16[192,1024]{1,0:T(8,128)(2,1)S(1)}, u32[]{:S(2)}) copy-start(bf16[192,1024]{1,0:T(8,128)(2,1)S(1)} %collective-permute-done.refs_1_) | copy-start | bytes 1179652
  20.9 22.9 %copy-start.4 = (bf16[192,1024]{1,0:T(8,128)(2,1)}, bf16[192,1024]{1,0:T(8,128)(2,1)S(1)}, u32[]{:S(2)}) copy-start(bf16[192,1024]{1,0:T(8,128)(2,1)S(1)} %collective-permute-done.1.refs_4_) | copy-start | bytes 1179652
  21.8 22.0 %copy-start.8 = (bf16[192,1024]{1,0:T(8,128)(2,1)}, bf16[192,1024]{1,0:T(8,128)(2,1)S(1)}, u32[]{:S(2)}) copy-start(bf16[192,1024]{1,0:T(8,128)(2,1)S(1)} %collective-permute-done.2.refs_5_) | copy-start | bytes 1179652
  21.8 10.0 %collective-permute-start.5 = (bf16[192,1024]{1,0:T(8,128)(2,1)S(1)}, bf16[192,1024]{1,0:T(8,128)(2,1)S(1)}, u32[]{:S(2)}, u32[]{:S(2)}) collective-permute-start(bf16[192,1024]{1,0:T(8,128)(2,1)S(1)} %collective-permute-done.2.refs_5_), channel_id=1, source_target_pairs={{0,4},{4,8},{8,12},{12,0},{1,5},{5,9},{9,13},{13,1},{2,6},{6,10},{... | collective-permute-start | bytes 1179656 | tf_op jit(solution)/shard_map/ppermute | solution.py:301
  21.8 10.1 %collective-permute-start.7 = (bf16[192,1024]{1,0:T(8,128)(2,1)S(1)}, bf16[192,1024]{1,0:T(8,128)(2,1)S(1)}, u32[]{:S(2)}, u32[]{:S(2)}) collective-permute-start(bf16[192,1024]{1,0:T(8,128)(2,1)S(1)} %collective-permute-done.2.refs_5_), channel_id=1, source_target_pairs={{0,12},{4,0},{8,4},{12,8},{1,13},{5,1},{9,5},{13,9},{2,14},{6,2},{... | collective-permute-start | bytes 1179656 | tf_op jit(solution)/shard_map/ppermute | solution.py:301
  24.5 19.2 %collective-permute-start.3 = (bf16[96,1024]{1,0:T(8,128)(2,1)S(1)}, bf16[96,1024]{1,0:T(8,128)(2,1)S(1)}, u32[]{:S(2)}, u32[]{:S(2)}) collective-permute-start(bf16[96,1024]{1,0:T(8,128)(2,1)S(1)} %slice.12), channel_id=1, source_target_pairs={{0,4},{4,8},{8,12},{12,0},{1,5},{5,9},{9,13},{13,1},{2,6},{6,10},{... | collective-permute-start | bytes 589832 | tf_op jit(solution)/shard_map/ppermute | solution.py:301
  24.6 19.1 %collective-permute-start.4 = (bf16[96,1024]{1,0:T(8,128)(2,1)S(1)}, bf16[96,1024]{1,0:T(8,128)(2,1)S(1)}, u32[]{:S(2)}, u32[]{:S(2)}) collective-permute-start(bf16[96,1024]{1,0:T(8,128)(2,1)S(1)} %slice.13), channel_id=1, source_target_pairs={{0,12},{4,0},{8,4},{12,8},{1,13},{5,1},{9,5},{13,9},{2,14},{6,2},{... | collective-permute-start | bytes 589832 | tf_op jit(solution)/shard_map/ppermute | solution.py:301
  31.8 12.0 %copy-start.5 = (bf16[192,1024]{1,0:T(8,128)(2,1)}, bf16[192,1024]{1,0:T(8,128)(2,1)S(1)}, u32[]{:S(2)}) copy-start(bf16[192,1024]{1,0:T(8,128)(2,1)S(1)} %collective-permute-done.5.refs_6_) | copy-start | bytes 1179652
  31.8 11.9 %collective-permute-start.6 = (bf16[96,1024]{1,0:T(8,128)(2,1)S(1)}, bf16[96,1024]{1,0:T(8,128)(2,1)S(1)}, u32[]{:S(2)}, u32[]{:S(2)}) collective-permute-start(bf16[96,1024]{1,0:T(8,128)(2,1)S(1)} %slice.16), channel_id=1, source_target_pairs={{0,4},{4,8},{8,12},{12,0},{1,5},{5,9},{9,13},{13,1},{2,6},{6,10},{... | collective-permute-start | bytes 589832 | tf_op jit(solution)/shard_map/ppermute | solution.py:301
  31.9 11.9 %copy-start.6 = (bf16[192,1024]{1,0:T(8,128)(2,1)}, bf16[192,1024]{1,0:T(8,128)(2,1)S(1)}, u32[]{:S(2)}) copy-start(bf16[192,1024]{1,0:T(8,128)(2,1)S(1)} %collective-permute-done.7.refs_9_) | copy-start | bytes 1179652
  31.9 11.8 %collective-permute-start.8 = (bf16[96,1024]{1,0:T(8,128)(2,1)S(1)}, bf16[96,1024]{1,0:T(8,128)(2,1)S(1)}, u32[]{:S(2)}, u32[]{:S(2)}) collective-permute-start(bf16[96,1024]{1,0:T(8,128)(2,1)S(1)} %slice.17), channel_id=1, source_target_pairs={{0,12},{4,0},{8,4},{12,8},{1,13},{5,1},{9,5},{13,9},{2,14},{6,2},{... | collective-permute-start | bytes 589832 | tf_op jit(solution)/shard_map/ppermute | solution.py:301
  43.7 1.1 copy-start.7
  43.7 1.1 copy-start.9
  43.7 1.2 copy-start.10
  43.7 1.2 copy-start.11
  43.8 1.3 copy-start.12
  55.1 6.0 %collective-permute-start.10 = (bf16[8,192,640]{2,1,0:T(8,128)(2,1)}, bf16[8,192,640]{2,1,0:T(8,128)(2,1)S(1)}, u32[]{:S(2)}, u32[]{:S(2)}) collective-permute-start(bf16[8,192,640]{2,1,0:T(8,128)(2,1)} %get-tuple-element.23), channel_id=1, source_target_pairs={{0,16},{16,0},{1,17},{17,1},{2,18},{18,2},{3,19},{19,3},{4,20},{20... | collective-permute-start | bytes 5898248 | tf_op jit(solution)/shard_map/ppermute | solution.py:347
  61.2 1.5 copy-start.2
  64.7 37.1 %all-to-all-start = ((bf16[64,24,640]{2,1,0:T(8,128)(2,1)}), bf16[64,24,640]{2,1,0:T(8,128)(2,1)S(1)}, u32[]{:S(2)}, u32[]{:S(2)}) async-start(bf16[64,24,640]{2,1,0:T(8,128)(2,1)} %bitcast.2), calls=%async_computation | async-start | bytes 3932160 | tf_op jit(solution)/shard_map/all_to_all | solution.py:349
  102.5 3.2 %collective-permute-start.11 = (bf16[4,2,24,640]{3,2,1,0:T(8,128)(2,1)S(1)}, bf16[4,2,24,640]{3,2,1,0:T(8,128)(2,1)S(1)}, u32[]{:S(2)}, u32[]{:S(2)}) collective-permute-start(bf16[4,2,24,640]{3,2,1,0:T(8,128)(2,1)S(1)} %get-tuple-element.29), channel_id=1, source_target_pairs={{0,16},{16,0},{1,17},{17,1},{2,18},{18,2},{3,19},{19,3},{4,20},{20... | collective-permute-start | bytes 737288 | tf_op jit(solution)/shard_map/ppermute | solution.py:354
  149.4 7.3 %collective-permute-start.12 = (bf16[384,2048]{1,0:T(8,128)(2,1)S(1)}, bf16[384,2048]{1,0:T(8,128)(2,1)S(1)}, u32[]{:S(2)}, u32[]{:S(2)}) collective-permute-start(bf16[384,2048]{1,0:T(8,128)(2,1)S(1)} %bitcast.19), channel_id=1, source_target_pairs={{0,16},{16,0},{1,17},{17,1},{2,18},{18,2},{3,19},{19,3},{4,20},{20... | collective-permute-start | bytes 4718600 | tf_op jit(solution)/shard_map/ppermute | solution.py:362
  151.5 2.2 %copy-start = (bf16[2048,1024]{1,0:T(8,128)(2,1)S(1)}, bf16[2048,1024]{1,0:T(8,128)(2,1)}, u32[]{:S(2)}) copy-start(bf16[2048,1024]{1,0:T(8,128)(2,1)} %all-gather.2.cloned.1.call-done.weight_ref) | copy-start | bytes 12582916
  153.7 3.0 %copy-start.1 = (bf16[2048,1024]{1,0:T(8,128)(2,1)S(1)}, bf16[2048,1024]{1,0:T(8,128)(2,1)}, u32[]{:S(2)}) copy-start(bf16[2048,1024]{1,0:T(8,128)(2,1)} %all-gather.2.cloned.1.call-done.weight_ref) | copy-start | bytes 12582916
Sparse Core Ops, SparseCore 0:
  57.5 67.9 all-gather.1

commit v5 on v4

--- a/solution.py
+++ b/solution.py
@@ -147,7 +147,7 @@
             jax.ShapeDtypeStruct((copies, groups, prompts, beams, given), jnp.bfloat16),
             jax.ShapeDtypeStruct((prompts, beams, width), jnp.bfloat16),
         ],
-        compiler_params=pltpu.CompilerParams(vmem_limit_bytes=56 * 1024 * 1024),
+        compiler_params=pltpu.CompilerParams(vmem_limit_bytes=50 * 1024 * 1024),
         cost_estimate=pl.CostEstimate(
             flops=4 * prompts * 64 * HEAD_SIZE * KEY_HEADS * (context + past),
             bytes_accessed=2 * prompts * width * (context + past),

time: 193 us -> 192 us (level)
    unnamed x26 -> x30, local copies, waits for them, and re-layouts: 4.98 us -> 4.99 us
  transfers between devices with their start and end apart: 15 -> 15, of which waited for: 7 -> 7; matrix products, arithmetic and copies ran while one was open for 2% -> 1% of each run, Pallas kernels for 10% -> 9%
where the time goes in v5:
time: 192 us
  blocking collectives  54.5 us (28%)
  waiting for transfers between devices  52.9 us (28%)
  Pallas kernels  31.3 us (16%)
  starting transfers between devices  30.5 us (16%)
  between operations  14.3 us (7%)
  local copies, waits for them, and re-layouts  5.88 us (3%)
  other arithmetic  2.36 us (1%)
    all_to_all x1, waiting for transfers between devices, body(): lax.all_to_all(terms, ('x', 'z', 'y'), split_axis=0, concat_axis=0, tiled...  29.3 us
    all_to_all x1, blocking collectives, body(): lax.all_to_all(copies, ('x', 'z'), split_axis=0, concat_axis=0, tiled=True)  29.1 us
    all_to_all x1, blocking collectives, body(): lax.all_to_all(product, ('z', 'y'), split_axis=0, concat_axis=0, tiled=True)  25.4 us
    pallas_call x1, Pallas kernels, attend(): pl.pallas_call(attend_kernel, grid_spec=grid_spec, out_shape=[jax.ShapeDt...  13.1 us
    ppermute x8, starting transfers between devices, shifted(): lax.ppermute(value, axis, [(i, (i + shift) % size) for i in range(size)])  13 us
    pallas_call x1, Pallas kernels, project(): pl.pallas_call(project_kernel, in_specs=[scalars, scalars] + [far] * (len...  10.1 us
    ppermute x1, waiting for transfers between devices, body(): other = lax.ppermute(qkv_weight, 'y', [(i, ny - 1 - i) for i in range(ny)])  9.06 us
    ppermute x8, waiting for transfers between devices, shifted(): lax.ppermute(value, axis, [(i, (i + shift) % size) for i in range(size)])  8.72 us
  transfers between devices with their start and end apart: 15, of which 7 were waited for; matrix products, arithmetic and copies ran while one was open for 1% of the time, Pallas kernels for 9%

profile of v5, /device:TPU:1, one launch (start us, length us, event | category | flops | bytes accessed | tf_op | source)
XLA Modules:
  0.0 191.7 jit_solution(17942344521203593291)
XLA Ops:
  7.2 2.5 %collective-permute-start = (bf16[192,1024]{1,0:T(8,128)(2,1)}, bf16[192,1024]{1,0:T(8,128)(2,1)S(1)}, u32[]{:S(2)}, u32[]{:S(2)}) collective-permute-start(bf16[192,1024]{1,0:T(8,128)(2,1)} %refs_0_), channel_id=1, source_target_pairs={{0,4},{4,8},{8,12},{12,0},{1,5},{5,9},{9,13},{13,1},{2,6},{6,10},{... | collective-permute-start | bytes 1179656 | tf_op jit(solution)/shard_map/ppermute | solution.py:301
  9.7 2.2 %collective-permute-start.1 = (bf16[192,1024]{1,0:T(8,128)(2,1)}, bf16[192,1024]{1,0:T(8,128)(2,1)S(1)}, u32[]{:S(2)}, u32[]{:S(2)}) collective-permute-start(bf16[192,1024]{1,0:T(8,128)(2,1)} %refs_0_), channel_id=1, source_target_pairs={{0,12},{4,0},{8,4},{12,8},{1,13},{5,1},{9,5},{13,9},{2,14},{6,2},{... | collective-permute-start | bytes 1179656 | tf_op jit(solution)/shard_map/ppermute | solution.py:301
  11.9 1.3 collective-permute-start.2
  13.2 1.9 collective-permute-start.9
  15.1 0.7 add_convert_fusion
  16.1 0.6 pad_add_fusion.places_ref
  16.6 4.3 %collective-permute-done.refs_1_ = bf16[192,1024]{1,0:T(8,128)(2,1)S(1)} collective-permute-done((bf16[192,1024]{1,0:T(8,128)(2,1)}, bf16[192,1024]{1,0:T(8,128)(2,1)S(1)}, u32[]{:S(2)}, u32[]{:S(2)}) %collective-permute-start) | collective-permute-done | bytes 393248 | tf_op jit(solution)/shard_map/ppermute | solution.py:301
  20.9 0.9 collective-permute-done.2.refs_5_
  21.8 2.7 %collective-permute-start.7 = (bf16[192,1024]{1,0:T(8,128)(2,1)S(1)}, bf16[192,1024]{1,0:T(8,128)(2,1)S(1)}, u32[]{:S(2)}, u32[]{:S(2)}) collective-permute-start(bf16[192,1024]{1,0:T(8,128)(2,1)S(1)} %collective-permute-done.2.refs_5_), channel_id=1, source_target_pairs={{0,12},{4,0},{8,4},{12,8},{1,13},{5,1},{9,5},{13,9},{2,14},{6,2},{... | collective-permute-start | bytes 1179656 | tf_op jit(solution)/shard_map/ppermute | solution.py:301
  24.6 2.7 %collective-permute-start.4 = (bf16[96,1024]{1,0:T(8,128)(2,1)S(1)}, bf16[96,1024]{1,0:T(8,128)(2,1)S(1)}, u32[]{:S(2)}, u32[]{:S(2)}) collective-permute-start(bf16[96,1024]{1,0:T(8,128)(2,1)S(1)} %slice.13), channel_id=1, source_target_pairs={{0,12},{4,0},{8,4},{12,8},{1,13},{5,1},{9,5},{13,9},{2,14},{6,2},{... | collective-permute-start | bytes 589832 | tf_op jit(solution)/shard_map/ppermute | solution.py:301
  27.4 4.4 %collective-permute-done.5.refs_6_ = bf16[192,1024]{1,0:T(8,128)(2,1)S(1)} collective-permute-done((bf16[192,1024]{1,0:T(8,128)(2,1)S(1)}, bf16[192,1024]{1,0:T(8,128)(2,1)S(1)}, u32[]{:S(2)}, u32[]{:S(2)}) %collective-permute-start.5) | collective-permute-done | bytes 393248 | tf_op jit(solution)/shard_map/ppermute | solution.py:301
  31.9 2.7 %collective-permute-start.8 = (bf16[96,1024]{1,0:T(8,128)(2,1)S(1)}, bf16[96,1024]{1,0:T(8,128)(2,1)S(1)}, u32[]{:S(2)}, u32[]{:S(2)}) collective-permute-start(bf16[96,1024]{1,0:T(8,128)(2,1)S(1)} %slice.17), channel_id=1, source_target_pairs={{0,12},{4,0},{8,4},{12,8},{1,13},{5,1},{9,5},{13,9},{2,14},{6,2},{... | collective-permute-start | bytes 589832 | tf_op jit(solution)/shard_map/ppermute | solution.py:301
  34.6 9.1 %collective-permute-done.9.refs_11_ = bf16[1024,640]{1,0:T(8,128)(2,1)S(1)} collective-permute-done((bf16[1024,640]{1,0:T(8,128)(2,1)}, bf16[1024,640]{1,0:T(8,128)(2,1)S(1)}, u32[]{:S(2)}, u32[]{:S(2)}) %collective-permute-start.9) | collective-permute-done | bytes 1310752 | tf_op jit(solution)/shard_map/ppermute | solution.py:323
  43.8 1.0 copy-done.9
  45.0 10.1 %shard_map.86 = (bf16[8,192,640]{2,1,0:T(8,128)(2,1)}, bf16[8,192,640]{2,1,0:T(8,128)(2,1)}) custom-call(s32[1]{0:T(128)} %bitcast.1.core_ref, s32[8]{0:T(128)} %pad_add_fusion.places_ref, bf16[192,1024]{1,0:T(8,128)(2,1)} %refs_0_, bf16[192,1024]{1,0:T(8,128)(2,1)} %copy-done.5, bf16[96,1024]{1,0:T(8,128)(2,1)} %copy-done.11, bf16[96,1024]{1,0:T(8,128)(2,1)} %copy-done.12, ...), custom_call_target="tpu_custom_call" | custom-call | flops 4026531840 | bytes 9699328 | tf_op jit(solution)/shard_map/pallas_call | solution.py:213
  55.1 2.2 %collective-permute-start.10 = (bf16[8,192,640]{2,1,0:T(8,128)(2,1)}, bf16[8,192,640]{2,1,0:T(8,128)(2,1)S(1)}, u32[]{:S(2)}, u32[]{:S(2)}) collective-permute-start(bf16[8,192,640]{2,1,0:T(8,128)(2,1)} %get-tuple-element.23), channel_id=1, source_target_pairs={{0,16},{16,0},{1,17},{17,1},{2,18},{18,2},{3,19},{19,3},{4,20},{20... | collective-permute-start | bytes 5898248 | tf_op jit(solution)/shard_map/ppermute | solution.py:347
  57.4 3.8 %collective-permute-done.10.b_ref = bf16[8,192,640]{2,1,0:T(8,128)(2,1)S(1)} collective-permute-done((bf16[8,192,640]{2,1,0:T(8,128)(2,1)}, bf16[8,192,640]{2,1,0:T(8,128)(2,1)S(1)}, u32[]{:S(2)}, u32[]{:S(2)}) %collective-permute-start.10) | collective-permute-done | bytes 1966112 | tf_op jit(solution)/shard_map/ppermute | solution.py:347
  61.2 1.5 copy-done.2
  62.7 2.1 %shard_map.87 = bf16[8,192,640]{2,1,0:T(8,128)(2,1)} custom-call(bf16[8,192,640]{2,1,0:T(8,128)(2,1)S(1)} %copy-done.2, bf16[8,192,640]{2,1,0:T(8,128)(2,1)S(1)} %collective-permute-done.10.b_ref), custom_call_target="tpu_custom_call" | custom-call | flops 983040 | bytes 5898240 | tf_op jit(solution)/shard_map/pallas_call | solution.py:244
  64.8 7.9 %all-to-all-start = ((bf16[64,24,640]{2,1,0:T(8,128)(2,1)}), bf16[64,24,640]{2,1,0:T(8,128)(2,1)S(1)}, u32[]{:S(2)}, u32[]{:S(2)}) async-start(bf16[64,24,640]{2,1,0:T(8,128)(2,1)} %bitcast.2), calls=%async_computation | async-start | bytes 3932160 | tf_op jit(solution)/shard_map/all_to_all | solution.py:349
  72.7 29.3 %all-to-all-done = bf16[64,24,640]{2,1,0:T(8,128)(2,1)S(1)} async-done(((bf16[64,24,640]{2,1,0:T(8,128)(2,1)}), bf16[64,24,640]{2,1,0:T(8,128)(2,1)S(1)}, u32[]{:S(2)}, u32[]{:S(2)}) %all-to-all-start) | async-done | bytes 1966112 | tf_op jit(solution)/shard_map/all_to_all | solution.py:349
  102.0 0.5 reduce_sum.24
  102.6 2.1 %collective-permute-start.11 = (bf16[4,2,24,640]{3,2,1,0:T(8,128)(2,1)S(1)}, bf16[4,2,24,640]{3,2,1,0:T(8,128)(2,1)S(1)}, u32[]{:S(2)}, u32[]{:S(2)}) collective-permute-start(bf16[4,2,24,640]{3,2,1,0:T(8,128)(2,1)S(1)} %get-tuple-element.29), channel_id=1, source_target_pairs={{0,16},{16,0},{1,17},{17,1},{2,18},{18,2},{3,19},{19,3},{4,20},{20... | collective-permute-start | bytes 737288 | tf_op jit(solution)/shard_map/ppermute | solution.py:354
  104.7 1.1 collective-permute-done.11
  105.9 13.1 %shard_map.88 = (bf16[4,4,3,8,2048]{4,3,2,1,0:T(8,128)(2,1)S(1)}, bf16[3,8,2048]{2,1,0:T(8,128)(2,1)}) custom-call(s32[24]{0:T(128)S(1)} %copy-done.3, s32[3]{0:T(128)S(1)} %copy-done.4, s32[16]{0:T(128)S(1)} %fusion.sources_ref, bf16[16,3,8,640]{3,2,1,0:T(8,128)(2,1)S(1)} %bitcast.21, f32[6,1,128]{2,1,0:T(1,128)S(1)} %broadcast_in_dim.11.cos_ref.sin_ref, ...), custom_call_target="tpu_custom_call" | custom-call | flops 1308622848 | bytes 20447232 | tf_op jit(solution)/shard_map/pallas_call | solution.py:143
  119.0 29.1 %all_to_all.15 = bf16[16,24,2048]{2,1,0:T(8,128)(2,1)S(1)} all-to-all(bf16[16,24,2048]{2,1,0:T(8,128)(2,1)S(1)} %bitcast.22), channel_id=1, replica_groups=mesh['x'=4,'core'=2,'z'=4,'y'=4] {'x','z'}, dimensions={0} | all-to-all | bytes 3145728 | tf_op jit(solution)/shard_map/all_to_all | solution.py:360
  148.1 2.1 %collective-permute-start.12 = (bf16[384,2048]{1,0:T(8,128)(2,1)S(1)}, bf16[384,2048]{1,0:T(8,128)(2,1)S(1)}, u32[]{:S(2)}, u32[]{:S(2)}) collective-permute-start(bf16[384,2048]{1,0:T(8,128)(2,1)S(1)} %bitcast.19), channel_id=1, source_target_pairs={{0,16},{16,0},{1,17},{17,1},{2,18},{18,2},{3,19},{19,3},{4,20},{20... | collective-permute-start | bytes 4718600 | tf_op jit(solution)/shard_map/ppermute | solution.py:362
  150.2 2.2 %copy-done = bf16[2048,1024]{1,0:T(8,128)(2,1)S(1)} copy-done((bf16[2048,1024]{1,0:T(8,128)(2,1)S(1)}, bf16[2048,1024]{1,0:T(8,128)(2,1)}, u32[]{:S(2)}) %copy-start) | copy-done | bytes 4194328
  152.4 3.0 %shard_map.89.refs_0_ = bf16[4,2,96,1024]{3,2,1,0:T(8,128)(2,1)S(1)} custom-call(s32[1]{0:T(128)} %bitcast.1.core_ref, bf16[384,2048]{1,0:T(8,128)(2,1)S(1)} %bitcast.20, bf16[2048,1024]{1,0:T(8,128)(2,1)S(1)} %copy-done), custom_call_target="tpu_custom_call" | custom-call | flops 1610612736 | bytes 6553600 | tf_op jit(solution)/shard_map/pallas_call | solution.py:282
  155.4 3.0 %shard_map.90 = bf16[4,2,96,1024]{3,2,1,0:T(8,128)(2,1)S(1)} custom-call(s32[1]{0:T(128)} %bitcast.core_ref, bf16[384,2048]{1,0:T(8,128)(2,1)S(1)} %collective-permute-done.12.rows_ref, bf16[2048,1024]{1,0:T(8,128)(2,1)S(1)} %copy-done.1, bf16[4,2,96,1024]{3,2,1,0:T(8,128)(2,1)S(1)} %shard_map.89.refs_0_), custom_call_target="tpu_custom_call", output_to_operand_aliasing={{}: (3, {})} | custom-call | flops 1610612736 | bytes 6553600 | tf_op jit(solution)/shard_map/pallas_call | solution.py:282
  158.4 25.4 %all_to_all.16 = bf16[16,48,1024]{2,1,0:T(8,128)(2,1)S(1)} all-to-all(bf16[16,48,1024]{2,1,0:T(8,128)(2,1)S(1)} %bitcast.18), channel_id=1, replica_groups=mesh['x'=4,'core'=2,'z'=4,'y'=4] {'z','y'}, dimensions={0} | all-to-all | bytes 3145728 | tf_op jit(solution)/shard_map/all_to_all | solution.py:366
  184.1 0.8 copy.10
  (53 shorter events, 1.2 us)
Async XLA Ops:
  7.2 143.0 %all-gather.2.cloned.1.call-start = ((), (), s32[]{:S(2)}) async-start(), calls=%async_computation.3 | async-start | bytes 5242880 | tf_op jit(solution)/shard_map/all_gather | solution.py:343
  7.2 13.7 %collective-permute-start = (bf16[192,1024]{1,0:T(8,128)(2,1)}, bf16[192,1024]{1,0:T(8,128)(2,1)S(1)}, u32[]{:S(2)}, u32[]{:S(2)}) collective-permute-start(bf16[192,1024]{1,0:T(8,128)(2,1)} %refs_0_), channel_id=1, source_target_pairs={{0,4},{4,8},{8,12},{12,0},{1,5},{5,9},{9,13},{13,1},{2,6},{6,10},{... | collective-permute-start | bytes 1179656 | tf_op jit(solution)/shard_map/ppermute | solution.py:301
  9.7 11.2 %collective-permute-start.1 = (bf16[192,1024]{1,0:T(8,128)(2,1)}, bf16[192,1024]{1,0:T(8,128)(2,1)S(1)}, u32[]{:S(2)}, u32[]{:S(2)}) collective-permute-start(bf16[192,1024]{1,0:T(8,128)(2,1)} %refs_0_), channel_id=1, source_target_pairs={{0,12},{4,0},{8,4},{12,8},{1,13},{5,1},{9,5},{13,9},{2,14},{6,2},{... | collective-permute-start | bytes 1179656 | tf_op jit(solution)/shard_map/ppermute | solution.py:301
  11.9 9.9 %collective-permute-start.2 = (bf16[192,1024]{1,0:T(8,128)(2,1)}, bf16[192,1024]{1,0:T(8,128)(2,1)S(1)}, u32[]{:S(2)}, u32[]{:S(2)}) collective-permute-start(bf16[192,1024]{1,0:T(8,128)(2,1)} %refs_0_), channel_id=1, source_target_pairs={{0,1},{1,0},{2,3},{3,2},{4,5},{5,4},{6,7},{7,6},{8,9},{9,8},{10,11... | collective-permute-start | bytes 1179656 | tf_op jit(solution)/shard_map/ppermute | solution.py:325
  13.2 30.5 %collective-permute-start.9 = (bf16[1024,640]{1,0:T(8,128)(2,1)}, bf16[1024,640]{1,0:T(8,128)(2,1)S(1)}, u32[]{:S(2)}, u32[]{:S(2)}) collective-permute-start(bf16[1024,640]{1,0:T(8,128)(2,1)} %refs_10_.1), channel_id=1, source_target_pairs={{0,3},{1,2},{2,1},{3,0},{4,7},{5,6},{6,5},{7,4},{8,11},{9,10},{10,... | collective-permute-start | bytes 3932168 | tf_op jit(solution)/shard_map/ppermute | solution.py:323
  20.9 22.8 %copy-start.5 = (bf16[192,1024]{1,0:T(8,128)(2,1)}, bf16[192,1024]{1,0:T(8,128)(2,1)S(1)}, u32[]{:S(2)}) copy-start(bf16[192,1024]{1,0:T(8,128)(2,1)S(1)} %collective-permute-done.refs_1_) | copy-start | bytes 1179652
  20.9 22.9 %copy-start.6 = (bf16[192,1024]{1,0:T(8,128)(2,1)}, bf16[192,1024]{1,0:T(8,128)(2,1)S(1)}, u32[]{:S(2)}) copy-start(bf16[192,1024]{1,0:T(8,128)(2,1)S(1)} %collective-permute-done.1.refs_4_) | copy-start | bytes 1179652
  21.8 22.0 %copy-start.10 = (bf16[192,1024]{1,0:T(8,128)(2,1)}, bf16[192,1024]{1,0:T(8,128)(2,1)S(1)}, u32[]{:S(2)}) copy-start(bf16[192,1024]{1,0:T(8,128)(2,1)S(1)} %collective-permute-done.2.refs_5_) | copy-start | bytes 1179652
  21.8 10.0 %collective-permute-start.5 = (bf16[192,1024]{1,0:T(8,128)(2,1)S(1)}, bf16[192,1024]{1,0:T(8,128)(2,1)S(1)}, u32[]{:S(2)}, u32[]{:S(2)}) collective-permute-start(bf16[192,1024]{1,0:T(8,128)(2,1)S(1)} %collective-permute-done.2.refs_5_), channel_id=1, source_target_pairs={{0,4},{4,8},{8,12},{12,0},{1,5},{5,9},{9,13},{13,1},{2,6},{6,10},{... | collective-permute-start | bytes 1179656 | tf_op jit(solution)/shard_map/ppermute | solution.py:301
  21.8 10.1 %collective-permute-start.7 = (bf16[192,1024]{1,0:T(8,128)(2,1)S(1)}, bf16[192,1024]{1,0:T(8,128)(2,1)S(1)}, u32[]{:S(2)}, u32[]{:S(2)}) collective-permute-start(bf16[192,1024]{1,0:T(8,128)(2,1)S(1)} %collective-permute-done.2.refs_5_), channel_id=1, source_target_pairs={{0,12},{4,0},{8,4},{12,8},{1,13},{5,1},{9,5},{13,9},{2,14},{6,2},{... | collective-permute-start | bytes 1179656 | tf_op jit(solution)/shard_map/ppermute | solution.py:301
  24.5 19.2 %collective-permute-start.3 = (bf16[96,1024]{1,0:T(8,128)(2,1)S(1)}, bf16[96,1024]{1,0:T(8,128)(2,1)S(1)}, u32[]{:S(2)}, u32[]{:S(2)}) collective-permute-start(bf16[96,1024]{1,0:T(8,128)(2,1)S(1)} %slice.12), channel_id=1, source_target_pairs={{0,4},{4,8},{8,12},{12,0},{1,5},{5,9},{9,13},{13,1},{2,6},{6,10},{... | collective-permute-start | bytes 589832 | tf_op jit(solution)/shard_map/ppermute | solution.py:301
  24.6 19.1 %collective-permute-start.4 = (bf16[96,1024]{1,0:T(8,128)(2,1)S(1)}, bf16[96,1024]{1,0:T(8,128)(2,1)S(1)}, u32[]{:S(2)}, u32[]{:S(2)}) collective-permute-start(bf16[96,1024]{1,0:T(8,128)(2,1)S(1)} %slice.13), channel_id=1, source_target_pairs={{0,12},{4,0},{8,4},{12,8},{1,13},{5,1},{9,5},{13,9},{2,14},{6,2},{... | collective-permute-start | bytes 589832 | tf_op jit(solution)/shard_map/ppermute | solution.py:301
  31.8 12.0 %copy-start.7 = (bf16[192,1024]{1,0:T(8,128)(2,1)}, bf16[192,1024]{1,0:T(8,128)(2,1)S(1)}, u32[]{:S(2)}) copy-start(bf16[192,1024]{1,0:T(8,128)(2,1)S(1)} %collective-permute-done.5.refs_6_) | copy-start | bytes 1179652
  31.8 11.9 %collective-permute-start.6 = (bf16[96,1024]{1,0:T(8,128)(2,1)S(1)}, bf16[96,1024]{1,0:T(8,128)(2,1)S(1)}, u32[]{:S(2)}, u32[]{:S(2)}) collective-permute-start(bf16[96,1024]{1,0:T(8,128)(2,1)S(1)} %slice.16), channel_id=1, source_target_pairs={{0,4},{4,8},{8,12},{12,0},{1,5},{5,9},{9,13},{13,1},{2,6},{6,10},{... | collective-permute-start | bytes 589832 | tf_op jit(solution)/shard_map/ppermute | solution.py:301
  31.9 11.9 %copy-start.8 = (bf16[192,1024]{1,0:T(8,128)(2,1)}, bf16[192,1024]{1,0:T(8,128)(2,1)S(1)}, u32[]{:S(2)}) copy-start(bf16[192,1024]{1,0:T(8,128)(2,1)S(1)} %collective-permute-done.7.refs_9_) | copy-start | bytes 1179652
  31.9 11.8 %collective-permute-start.8 = (bf16[96,1024]{1,0:T(8,128)(2,1)S(1)}, bf16[96,1024]{1,0:T(8,128)(2,1)S(1)}, u32[]{:S(2)}, u32[]{:S(2)}) collective-permute-start(bf16[96,1024]{1,0:T(8,128)(2,1)S(1)} %slice.17), channel_id=1, source_target_pairs={{0,12},{4,0},{8,4},{12,8},{1,13},{5,1},{9,5},{13,9},{2,14},{6,2},{... | collective-permute-start | bytes 589832 | tf_op jit(solution)/shard_map/ppermute | solution.py:301
  43.7 1.1 copy-start.9
  43.7 1.2 copy-start.11
  43.7 1.2 copy-start.12
  43.7 1.2 copy-start.13
  43.8 1.3 copy-start.14
  55.1 6.1 %collective-permute-start.10 = (bf16[8,192,640]{2,1,0:T(8,128)(2,1)}, bf16[8,192,640]{2,1,0:T(8,128)(2,1)S(1)}, u32[]{:S(2)}, u32[]{:S(2)}) collective-permute-start(bf16[8,192,640]{2,1,0:T(8,128)(2,1)} %get-tuple-element.23), channel_id=1, source_target_pairs={{0,16},{16,0},{1,17},{17,1},{2,18},{18,2},{3,19},{19,3},{4,20},{20... | collective-permute-start | bytes 5898248 | tf_op jit(solution)/shard_map/ppermute | solution.py:347
  61.2 1.5 copy-start.2
  64.8 37.1 %all-to-all-start = ((bf16[64,24,640]{2,1,0:T(8,128)(2,1)}), bf16[64,24,640]{2,1,0:T(8,128)(2,1)S(1)}, u32[]{:S(2)}, u32[]{:S(2)}) async-start(bf16[64,24,640]{2,1,0:T(8,128)(2,1)} %bitcast.2), calls=%async_computation | async-start | bytes 3932160 | tf_op jit(solution)/shard_map/all_to_all | solution.py:349
  102.0 3.9 %copy-start.3 = (s32[24]{0:T(128)S(1)}, s32[24]{0:T(128)}, u32[]{:S(2)}) copy-start(s32[24]{0:T(128)} %parents_ref.1) | copy-start | bytes 292
  102.0 3.9 %copy-start.4 = (s32[3]{0:T(128)S(1)}, s32[3]{0:T(128)}, u32[]{:S(2)}) copy-start(s32[3]{0:T(128)} %lengths_ref.1) | copy-start | bytes 40
  102.6 3.2 %collective-permute-start.11 = (bf16[4,2,24,640]{3,2,1,0:T(8,128)(2,1)S(1)}, bf16[4,2,24,640]{3,2,1,0:T(8,128)(2,1)S(1)}, u32[]{:S(2)}, u32[]{:S(2)}) collective-permute-start(bf16[4,2,24,640]{3,2,1,0:T(8,128)(2,1)S(1)} %get-tuple-element.29), channel_id=1, source_target_pairs={{0,16},{16,0},{1,17},{17,1},{2,18},{18,2},{3,19},{19,3},{4,20},{20... | collective-permute-start | bytes 737288 | tf_op jit(solution)/shard_map/ppermute | solution.py:354
  148.1 7.3 %collective-permute-start.12 = (bf16[384,2048]{1,0:T(8,128)(2,1)S(1)}, bf16[384,2048]{1,0:T(8,128)(2,1)S(1)}, u32[]{:S(2)}, u32[]{:S(2)}) collective-permute-start(bf16[384,2048]{1,0:T(8,128)(2,1)S(1)} %bitcast.19), channel_id=1, source_target_pairs={{0,16},{16,0},{1,17},{17,1},{2,18},{18,2},{3,19},{19,3},{4,20},{20... | collective-permute-start | bytes 4718600 | tf_op jit(solution)/shard_map/ppermute | solution.py:362
  150.2 2.2 %copy-start = (bf16[2048,1024]{1,0:T(8,128)(2,1)S(1)}, bf16[2048,1024]{1,0:T(8,128)(2,1)}, u32[]{:S(2)}) copy-start(bf16[2048,1024]{1,0:T(8,128)(2,1)} %all-gather.2.cloned.1.call-done.weight_ref) | copy-start | bytes 12582916
  152.4 3.0 %copy-start.1 = (bf16[2048,1024]{1,0:T(8,128)(2,1)S(1)}, bf16[2048,1024]{1,0:T(8,128)(2,1)}, u32[]{:S(2)}) copy-start(bf16[2048,1024]{1,0:T(8,128)(2,1)} %all-gather.2.cloned.1.call-done.weight_ref) | copy-start | bytes 12582916
Sparse Core Ops, SparseCore 0:
  57.5 67.9 all-gather.1
